TPU v7x, 128 devices: a whole 4x4x4 slice. The times are simulated.
128 devices in a mesh: grp: 4 (over y_hi, core), fsdp: 32 (over x, y_lo, z).
Axes of the slice: x: 4, y: 4 (y_hi: 2, y_lo: 2; y = y_hi * 2 + y_lo), z: 4, core: 2. Of those that a mesh axis runs over, the one named last changes fastest.
Arguments:
- small_w: bfloat16 [4, 4096, 4096], P('grp', 'fsdp'), may hold values from -0.09375 to 0.09375
- small_m: float32 [4, 4096, 4096], P('grp', 'fsdp'), may hold values from -6 to 6
- small_v: float32 [4, 4096, 4096], P('grp', 'fsdp'), may hold values from 0 to 1, as said below
- width_map: bfloat16 [2560, 4096], P(('grp', 'fsdp')), may hold values from -1 to 1
- head_map: float32 [40, 32], replicated, may hold values from -1 to 1
- layer_slot: int32 [4], replicated, may hold values from 0 to 3, each once
- depth_src: int32 [5, 2], replicated, may hold values from 0 to 3, as said below
- depth_coef: float32 [5, 2], replicated, may hold values from 0.3 to 1
Outputs:
- grown_w: bfloat16 [5, 5120, 2560], P(None, ('grp', 'fsdp'))
- grown_m: float32 [5, 5120, 2560], P(None, ('grp', 'fsdp'))
- grown_v: float32 [5, 5120, 2560], P(None, ('grp', 'fsdp'))
Inputs may be any that keep to these rules, and one draw needn't show every extreme that they name: `layer_slot`: each source layer fills exactly one slot. `depth_src`: the first source of grown layer j is j * 4 // 5. `small_v`: positive.
All inputs are finite; a program needn't handle non-finite values.
Results may differ from a plain program's by a relative error of at most 0.0057.
Values may be sent and summed in bfloat16 or wider, within the bound.
No kernel may reach another device: no remote copies, remote signals or barrier semaphores. Data moves between devices by JAX's collectives and lax.ppermute only.
A program may use at most 256 MiB of HBM per device.

v0:
```python
import jax
import jax.numpy as jnp
from jax import lax
from jax.sharding import PartitionSpec as P


def depth_matrix(layer_slot, depth_src, depth_coef):
    hits = (layer_slot[None, None, :] == depth_src[:, :, None]).astype(jnp.float32)
    return jnp.sum(depth_coef[:, :, None] * hits, axis=1)


def project(left, right, exact):
    dims = (((left.ndim - 1,), (1,)), ((), ()))
    if exact:
        return lax.dot_general(
            left, right, dims, precision=lax.Precision.HIGHEST, preferred_element_type=jnp.float32
        )
    return lax.dot_general(left, right, dims, preferred_element_type=jnp.float32)


def mix_heads(block, matrix):
    shape = block.shape
    heads = matrix.shape[1]
    split = block.reshape(shape[:-2] + (heads, shape[-2] // heads, shape[-1]))
    mixed = jnp.einsum("gh,...hdc->...gdc", matrix, split, precision=lax.Precision.HIGHEST)
    return mixed.reshape(shape[:-2] + (matrix.shape[0] * (shape[-2] // heads), shape[-1]))


def widen_panels(panels_w, panels_m, panels_v, piece):
    wide = piece.astype(jnp.float32)
    z_w = project(panels_w, piece, False)
    z_m = project(panels_m, wide, True)
    z_v = project(panels_v, wide * wide, True)
    return jnp.stack([z_w, z_m, z_v])


def grow_blocks(slab_w, slab_m, slab_v, head_map):
    y_w = mix_heads(slab_w.astype(jnp.float32), head_map).astype(jnp.bfloat16)
    y_m = mix_heads(slab_m, head_map)
    y_v = mix_heads(slab_v, head_map * head_map)
    return (y_w, y_m, y_v)


def mix_depth(depth, stack_w, stack_m, stack_v):
    hi = lax.Precision.HIGHEST
    grown_w = jnp.einsum("js,src->jrc", depth, stack_w.astype(jnp.float32), precision=hi).astype(
        jnp.bfloat16
    )
    grown_m = jnp.einsum("js,src->jrc", depth, stack_m, precision=hi)
    grown_v = jnp.einsum("js,src->jrc", depth * depth, stack_v, precision=hi)
    return (grown_w, grown_m, grown_v)


def on_device(small_w, small_m, small_v, width_map, head_map, layer_slot, depth_src, depth_coef):
    depth = depth_matrix(layer_slot, depth_src, depth_coef)
    n_grp = lax.axis_size("grp")
    n_fsdp = lax.axis_size("fsdp")
    stacked = widen_panels(
        small_w, small_m, small_v, lax.all_gather(width_map, ("grp", "fsdp"), axis=0, tiled=True)
    )
    z_w = stacked[0, 0].astype(jnp.bfloat16)
    slab_w, slab_m, slab_v = (
        lax.all_to_all(
            z_w.astype(jnp.float32), "fsdp", split_axis=1, concat_axis=0, tiled=True
        ).astype(z_w.dtype),
        lax.all_to_all(stacked[1, 0], "fsdp", split_axis=1, concat_axis=0, tiled=True),
        lax.all_to_all(stacked[2, 0], "fsdp", split_axis=1, concat_axis=0, tiled=True),
    )
    y_w, y_m, y_v = grow_blocks(slab_w, slab_m, slab_v, head_map)
    r_w, r_m, r_v = (
        lax.all_to_all(
            y_w[:, None, :].astype(jnp.float32),
            ("grp", "fsdp"),
            split_axis=0,
            concat_axis=1,
            tiled=True,
        ).astype(jnp.bfloat16),
        lax.all_to_all(y_m[:, None, :], ("grp", "fsdp"), split_axis=0, concat_axis=1, tiled=True),
        lax.all_to_all(y_v[:, None, :], ("grp", "fsdp"), split_axis=0, concat_axis=1, tiled=True),
    )
    owned_rows = r_w.shape[0]
    width = n_fsdp * r_w.shape[2]

    def regroup(block):
        return block.reshape(owned_rows, n_grp, width).transpose(1, 0, 2)

    grown_w, grown_m, grown_v = mix_depth(depth, regroup(r_w), regroup(r_m), regroup(r_v))
    return (grown_w, grown_m, grown_v)


def solution(mesh):
    return jax.shard_map(
        on_device,
        mesh=mesh,
        in_specs=(
            P("grp", "fsdp", None),
            P("grp", "fsdp", None),
            P("grp", "fsdp", None),
            P(("grp", "fsdp"), None),
            P(),
            P(),
            P(),
            P(),
        ),
        out_specs=(
            P(None, ("grp", "fsdp"), None),
            P(None, ("grp", "fsdp"), None),
            P(None, ("grp", "fsdp"), None),
        ),
        check_vma=False,
    )
```

profile of v0, /device:TPU:1, one launch (start us, length us, event | category | flops | bytes accessed | tf_op | source)
XLA Modules:
  0.0 730.2 jit_solution(17798926388489488351)
XLA Ops:
  7.9 344.0 %all-gather.3.cloned.1.call-done = bf16[128,20,4096]{2,1,0:T(8,128)(2,1)} async-done(((bf16[1,20,4096]{2,1,0:T(8,128)(2,1)}), bf16[128,20,4096]{2,1,0:T(8,128)(2,1)}) %all-gather.3.cloned.1.call-update) | async-done | bytes 20971536 | tf_op jit(solution)/shard_map/all_gather | solution.py:59
  351.9 26.5 %dot_general.33 = bf16[32,80,4096]{2,1,0:T(8,128)(2,1)} reshape(bf16[128,20,4096]{2,1,0:T(8,128)(2,1)} %all-gather.3.cloned.1.call-done) | data formatting | bytes 41943040 | tf_op jit(solution)/shard_map/dot_general | solution.py:18
  378.4 23.7 %fusion.13 = bf16[128,32,80]{0,1,2:T(8,128)(2,1)S(1)} fusion(bf16[32,80,4096]{2,1,0:T(8,128)(2,1)} %dot_general.33, bf16[1,128,4096]{2,1,0:T(8,128)(2,1)S(1)} %copy-done.8), kind=kOutput, calls=%fused_computation.16 | convolution fusion | flops 2684682240 | bytes 22675456 | tf_op jit(solution)/shard_map/dot_general | solution.py:18
  403.3 7.4 %all-to-all-start = ((bf16[128,32,80]{0,2,1:T(8,128)(2,1)}), bf16[128,32,80]{0,2,1:T(8,128)(2,1)S(1)}, u32[]{:S(2)}, u32[]{:S(2)}) async-start(bf16[128,32,80]{0,2,1:T(8,128)(2,1)} %copy.51), calls=%async_computation | async-start | bytes 1310720 | tf_op jit(solution)/shard_map/all_to_all | solution.py:63
  410.7 27.5 %convert_multiply_fusion = f32[128,20,4096]{2,1,0:T(8,128)} fusion(bf16[128,20,4096]{2,1,0:T(8,128)(2,1)} %all-gather.3.cloned.1.call-done), kind=kLoop, calls=%fused_computation | loop fusion | flops 20971520 | bytes 62914560 | tf_op jit(solution)/shard_map/mul | solution.py:33
  438.2 20.4 %fusion.4 = f32[128,32,80]{0,2,1:T(8,128)} fusion(bf16[32,80,4096]{2,1,0:T(8,128)(2,1)} %dot_general.33, f32[1,128,4096]{2,1,0:T(8,128)S(1)} %copy-done), kind=kOutput, calls=%fused_computation.6 | convolution fusion | flops 16106127360 | bytes 24379392 | tf_op jit(solution)/shard_map/dot_general | solution.py:15
  458.6 41.6 %reshape.81 = f32[2560,4096]{1,0:T(8,128)} reshape(f32[128,20,4096]{2,1,0:T(8,128)} %convert_multiply_fusion) | data formatting | bytes 83886080 | tf_op jit(solution)/shard_map/mul | solution.py:33
  500.2 7.8 %all-to-all-start.2 = ((f32[128,32,80]{0,2,1:T(8,128)}), f32[128,32,80]{0,2,1:T(8,128)S(1)}, u32[]{:S(2)}, u32[]{:S(2)}) async-start(f32[128,32,80]{0,2,1:T(8,128)} %fusion.4), calls=%async_computation.2 | async-start | bytes 2621440 | tf_op jit(solution)/shard_map/all_to_all | solution.py:66
  508.0 38.0 %fusion.2 = f32[2560,128]{1,0:T(8,128)} fusion(f32[2560,4096]{1,0:T(8,128)} %reshape.81, f32[1,128,4096]{2,1,0:T(8,128)} %param.10), kind=kOutput, calls=%fused_computation.4 | convolution fusion | flops 16106127360 | bytes 45350912 | tf_op jit(solution)/shard_map/dot_general | solution.py:15
  547.1 7.7 %all-to-all-start.4 = ((f32[128,32,80]{0,2,1:T(8,128)}), f32[128,32,80]{0,2,1:T(8,128)S(1)}, u32[]{:S(2)}, u32[]{:S(2)}) async-start(f32[128,32,80]{0,2,1:T(8,128)} %bitcast.22), calls=%async_computation.4 | async-start | bytes 2621440 | tf_op jit(solution)/shard_map/all_to_all | solution.py:67
  556.8 2.1 copy.68
  558.9 5.4 convert.2
  564.9 28.9 %reduce = bf16[5120,80]{1,0:T(8,128)(2,1)S(1)} reduce(bf16[5120,1,80]{2,1,0:T(2,128)(2,1)} %convert.2, bf16[]{:T(256)} %broadcast.8), dimensions={1}, to_apply=%convert.2.reduce_sub_computation | reduce | bytes 1638402
  593.7 3.3 reshape.88
  597.1 10.8 %all-to-all-start.1 = ((bf16[128,2,1600]{2,1,0:T(2,128)(2,1)}), bf16[128,2,1600]{2,1,0:T(2,128)(2,1)}, u32[]{:S(2)}, u32[]{:S(2)}) async-start(bf16[128,2,1600]{2,1,0:T(2,128)(2,1)} %reshape.88), calls=%async_computation.1 | async-start | bytes 1703936 | tf_op jit(solution)/shard_map/all_to_all | solution.py:71
  607.9 3.3 convolution_bitcast_fusion
  611.1 2.1 copy.69
  613.2 11.2 %all-to-all-done.1 = bf16[128,2,1600]{2,1,0:T(2,128)(2,1)} async-done(((bf16[128,2,1600]{2,1,0:T(2,128)(2,1)}), bf16[128,2,1600]{2,1,0:T(2,128)(2,1)}, u32[]{:S(2)}, u32[]{:S(2)}) %all-to-all-start.1) | async-done | bytes 819232 | tf_op jit(solution)/shard_map/all_to_all | solution.py:71
  624.4 6.1 all-to-all-start.3
  632.2 2.2 copy.70
  634.3 31.6 %all-to-all-done.3 = f32[5120,1,80]{2,1,0:T(1,128)} async-done(((f32[5120,1,80]{2,1,0:T(1,128)}), f32[5120,1,80]{2,1,0:T(1,128)}, u32[]{:S(2)}, u32[]{:S(2)}) %all-to-all-start.3) | async-done | bytes 1638432 | tf_op jit(solution)/shard_map/all_to_all | solution.py:78
  665.9 5.7 all-to-all-start.5
  671.7 10.0 %reshape.89 = bf16[5120,1,80]{2,1,0:T(2,128)(2,1)} reshape(bf16[128,2,1600]{2,1,0:T(2,128)(2,1)} %all-to-all-done.1) | data formatting | bytes 1638400
  689.2 3.8 copy.59
  693.0 3.4 reshape.73
  696.4 3.6 fusion.8
  700.0 2.5 copy.64
  702.5 4.7 all-to-all-done.5
  707.2 3.8 copy.62
  711.0 4.5 reshape.75
  715.4 5.2 fusion.6
  720.7 2.5 copy.65
  (33 shorter events, 14.5 us)
Async XLA Ops:
  7.2 431.0 %copy-start = (f32[1,128,4096]{2,1,0:T(8,128)S(1)}, f32[1,128,4096]{2,1,0:T(8,128)}, u32[]{:S(2)}) copy-start(f32[1,128,4096]{2,1,0:T(8,128)} %param.9) | copy-start | bytes 6291460
  7.2 344.7 %all-gather.3.cloned.1.call-start = ((), (), s32[]{:S(2)}) async-start(), calls=%async_computation.6 | async-start | bytes 25362432 | tf_op jit(solution)/shard_map/all_gather | solution.py:59
  7.9 370.5 %copy-start.8 = (bf16[1,128,4096]{2,1,0:T(8,128)(2,1)S(1)}, bf16[1,128,4096]{2,1,0:T(8,128)(2,1)}, u32[]{:S(2)}) copy-start(bf16[1,128,4096]{2,1,0:T(8,128)(2,1)} %param.8) | copy-start | bytes 3145732
  403.3 96.9 %all-to-all-start = ((bf16[128,32,80]{0,2,1:T(8,128)(2,1)}), bf16[128,32,80]{0,2,1:T(8,128)(2,1)S(1)}, u32[]{:S(2)}, u32[]{:S(2)}) async-start(bf16[128,32,80]{0,2,1:T(8,128)(2,1)} %copy.51), calls=%async_computation | async-start | bytes 1310720 | tf_op jit(solution)/shard_map/all_to_all | solution.py:63
  500.2 45.8 %copy-start.3 = (bf16[128,32,80]{0,2,1:T(8,128)(2,1)}, bf16[128,32,80]{0,2,1:T(8,128)(2,1)S(1)}, u32[]{:S(2)}) copy-start(bf16[128,32,80]{0,2,1:T(8,128)(2,1)S(1)} %all-to-all-done) | copy-start | bytes 1966084
  500.2 45.8 %all-to-all-start.2 = ((f32[128,32,80]{0,2,1:T(8,128)}), f32[128,32,80]{0,2,1:T(8,128)S(1)}, u32[]{:S(2)}, u32[]{:S(2)}) async-start(f32[128,32,80]{0,2,1:T(8,128)} %fusion.4), calls=%async_computation.2 | async-start | bytes 2621440 | tf_op jit(solution)/shard_map/all_to_all | solution.py:66
  546.0 8.8 %copy-start.4 = (f32[40,32]{0,1:T(8,128)S(1)}, f32[40,32]{0,1:T(8,128)}, u32[]{:S(2)}) copy-start(f32[40,32]{0,1:T(8,128)} %param.12) | copy-start | bytes 15364
  546.0 1.1 copy-start.2
  547.1 50.0 %all-to-all-start.4 = ((f32[128,32,80]{0,2,1:T(8,128)}), f32[128,32,80]{0,2,1:T(8,128)S(1)}, u32[]{:S(2)}, u32[]{:S(2)}) async-start(f32[128,32,80]{0,2,1:T(8,128)} %bitcast.22), calls=%async_computation.4 | async-start | bytes 2621440 | tf_op jit(solution)/shard_map/all_to_all | solution.py:67
  597.1 27.3 %all-to-all-start.1 = ((bf16[128,2,1600]{2,1,0:T(2,128)(2,1)}), bf16[128,2,1600]{2,1,0:T(2,128)(2,1)}, u32[]{:S(2)}, u32[]{:S(2)}) async-start(bf16[128,2,1600]{2,1,0:T(2,128)(2,1)} %reshape.88), calls=%async_computation.1 | async-start | bytes 1703936 | tf_op jit(solution)/shard_map/all_to_all | solution.py:71
  624.4 41.5 %all-to-all-start.3 = ((f32[5120,1,80]{2,1,0:T(1,128)}), f32[5120,1,80]{2,1,0:T(1,128)}, u32[]{:S(2)}, u32[]{:S(2)}) async-start(f32[5120,1,80]{2,1,0:T(1,128)} %bitcast.80), calls=%async_computation.3 | async-start | bytes 5242880 | tf_op jit(solution)/shard_map/all_to_all | solution.py:78
  665.9 5.7 copy-start.5
  665.9 5.8 copy-start.6
  665.9 5.8 copy-start.7
  665.9 41.3 %all-to-all-start.5 = ((f32[5120,1,80]{2,1,0:T(1,128)}), f32[5120,1,80]{2,1,0:T(1,128)}, u32[]{:S(2)}, u32[]{:S(2)}) async-start(f32[5120,1,80]{2,1,0:T(1,128)} %bitcast.79), calls=%async_computation.5 | async-start | bytes 5242880 | tf_op jit(solution)/shard_map/all_to_all | solution.py:79
  715.4 7.7 %copy-start.1 = (f32[1,128,4096]{2,1,0:T(8,128)S(1)}, f32[1,128,4096]{2,1,0:T(8,128)}, u32[]{:S(2)}) copy-start(f32[1,128,4096]{2,1,0:T(8,128)} %param.9) | copy-start | bytes 6291460
Sparse Core Ops, SparseCore 0:
  9.7 342.1 all-gather.2
where the time goes:
time: 740 us; the launch traced here: 730 us
  waiting for transfers between devices  392 us (53%)
  local copies, waits for them, and re-layouts  117 us (16%)
  matrix products  99.6 us (13%)
  other arithmetic  61.9 us (8%)
  starting transfers between devices  45.6 us (6%)
  between operations  14.5 us (2%)
    all_gather x1, waiting for transfers between devices, on_device(): lax.all_gather(width_map, ('grp', 'fsdp'), axis=0, tiled=True)  344 us
    dot_general x2, matrix products, project(): lax.dot_general(left, right, dims, precision=lax.Precision.HIGHEST, prefe...  58.4 us
    mul x1, local copies, waits for them, and re-layouts, widen_panels(): z_v = project(panels_v, wide * wide, True)  41.6 us
    unnamed x2, other arithmetic  34.3 us
    all_to_all x1, waiting for transfers between devices, on_device(): lax.all_to_all(y_m[:, None, :], ('grp', 'fsdp'), split_axis=0, concat_axi...  31.6 us
    mul x1, other arithmetic, widen_panels(): z_v = project(panels_v, wide * wide, True)  27.5 us
    dot_general x1, local copies, waits for them, and re-layouts, project(): lax.dot_general(left, right, dims, preferred_element_type=jnp.float32)  26.5 us
    dot_general x1, matrix products, project(): lax.dot_general(left, right, dims, preferred_element_type=jnp.float32)  23.7 us
  transfers between devices with their start and end apart: 7, of which 4 were waited for; matrix products, arithmetic and copies ran while one was open for 29% of the time, Pallas kernels for 0%

commit v1 on v0

v1 whole, which is shorter than its diff:
```python
import jax
import jax.numpy as jnp
from jax import lax
from jax.experimental import pallas as pl
from jax.experimental.pallas import tpu as pltpu
from jax.sharding import Mesh, PartitionSpec as P

SIZES = (2, 2, 4, 2, 4)
AXES = ("yh", "core", "x", "yl", "z")
GROUP = ("x", "yl", "z")
BF16, F32 = jnp.bfloat16, jnp.float32

COLS, HALF, DEPTH = 2560, 1280, 4096
BLOCK = 80
UNITS = 64
VMEM = 56 * 1024 * 1024


def place(yh, core, x, yl, z):
    return (((yh * 2 + core) * 4 + x) * 2 + yl) * 4 + z


def shift(value, axis_of_core, by):
    pairs = []
    for yh in range(2):
        for core in range(2):
            for x in range(4):
                for yl in range(2):
                    for z in range(4):
                        to = [x, 2 * yh + yl]
                        to[axis_of_core[core]] = (to[axis_of_core[core]] + by) % 4
                        pairs.append(
                            (place(yh, core, x, yl, z), place(to[1] // 2, core, to[0], to[1] % 2, z))
                        )
    return lax.ppermute(value, AXES, pairs)


def gather_width(shard):
    block = lax.all_gather(shard, "z", axis=0, tiled=True)
    first, second = (1, 0), (0, 1)
    before, after, across = (
        shift(block, first, 1),
        shift(block, first, -1),
        shift(block, first, 2),
    )
    a = jnp.concatenate([block, before], axis=0)
    b = jnp.concatenate([after, across], axis=0)
    ra, lb = shift(a, second, 1), shift(b, second, -1)
    rb, la = shift(b, second, 1), shift(a, second, -1)
    pieces = [a, b, ra, rb, la, lb, shift(ra, second, 1), shift(lb, second, -1)]
    core = lax.axis_index("core")
    x = lax.axis_index("x")
    y = lax.axis_index("yh") * 2 + lax.axis_index("yl")
    rows = []
    for late in (0, -1, 1, 2):
        for early in (0, -1, 1, 2):
            bx = (x + jnp.where(core == 0, late, early)) % 4
            by = (y + jnp.where(core == 0, early, late)) % 4
            rows.append(((by // 2) * 8 + bx * 2 + by % 2) * BLOCK)
    return pieces, jnp.stack(rows).astype(jnp.int32)


def widen_kernel(rows, own, other, *refs):
    pieces, out = refs[:8], refs[8]
    b_ref, a_ref, b_sem, a_sem = refs[9:]
    copies = []
    for i, (src, dst) in enumerate(
        (
            (own.at[0:2], a_ref.at[0:2]),
            (other.at[0:2], a_ref.at[2:4]),
            (own.at[2:3], a_ref.at[4:5]),
            (other.at[2:3], a_ref.at[5:6]),
        )
    ):
        copies.append(pltpu.make_async_copy(src, dst, a_sem.at[i]))
    for i in range(16):
        copies.append(
            pltpu.make_async_copy(
                pieces[i // 2].at[pl.ds((i % 2) * BLOCK, BLOCK)],
                b_ref.at[pl.ds(pl.multiple_of(rows[i], 16), BLOCK)],
                b_sem.at[i],
            )
        )
    for copy in copies:
        copy.start()
    for copy in copies:
        copy.wait()
    nt = (((1,), (1,)), ((), ()))

    @pl.loop(0, HALF // 256)
    def _(tile):
        b = b_ref[pl.ds(pl.multiple_of(tile * 256, 256), 256), :]
        wm = lax.dot_general(
            a_ref[0:4].reshape(512, DEPTH), b, nt, preferred_element_type=F32
        ).astype(BF16)
        v = lax.dot_general(
            a_ref[4:6].reshape(256, DEPTH), b * b, nt, preferred_element_type=F32
        ).astype(BF16)
        for half in range(2):
            cols = slice(half * 128, half * 128 + 128)
            t = tile * 2 + half
            out[t] = wm[0:128, cols]
            out[10 + t] = wm[128:256, cols]
            out[20 + t] = v[0:128, cols]
            out[30 + t] = wm[256:384, cols]
            out[40 + t] = wm[384:512, cols]
            out[50 + t] = v[128:256, cols]

    out[60:64] = jnp.zeros((4, 128, 128), BF16)


def widen(rows, own, other, pieces):
    anywhere = pl.BlockSpec(memory_space=pl.ANY)
    return pl.pallas_call(
        widen_kernel,
        out_shape=jax.ShapeDtypeStruct((UNITS, 128, 128), BF16),
        in_specs=[pl.BlockSpec(memory_space=pltpu.SMEM)] + [anywhere] * 10,
        out_specs=pl.BlockSpec(memory_space=pltpu.VMEM),
        scratch_shapes=[
            pltpu.VMEM((HALF, DEPTH), BF16),
            pltpu.VMEM((6, 128, DEPTH), BF16),
            pltpu.SemaphoreType.DMA((16,)),
            pltpu.SemaphoreType.DMA((4,)),
        ],
        compiler_params=pltpu.CompilerParams(vmem_limit_bytes=VMEM),
        cost_estimate=pl.CostEstimate(
            flops=2 * 768 * HALF * DEPTH, bytes_accessed=20 << 20, transcendentals=0
        ),
        name="widen",
    )(rows, own, other, *pieces)


def mix_kernel(z_ref, m_ref, out, y_ref):
    for k in range(2):

        @pl.loop(0, 4)
        def _(pair):
            row = pl.multiple_of(pair * 32, 32)
            block = jnp.concatenate(
                [z_ref[:, k, pl.ds(row + 16 * i, 16), :].reshape(512, 128) for i in range(2)], axis=1
            )
            y = jnp.dot(m_ref[0], block, preferred_element_type=F32)
            y = y + jnp.dot(m_ref[1], block, preferred_element_type=F32)
            for g in range(40):
                for i in range(2):
                    y_ref[k, pl.ds(g * 128 + row + 16 * i, 16), :] = y[
                        g * 16 : g * 16 + 16, i * 128 : i * 128 + 128
                    ]

    @pl.loop(0, 128, unroll=4)
    def _(d):
        row = pl.multiple_of(d * 40, 8)
        both = jnp.concatenate([y_ref[k, pl.ds(row, 40), :] for k in range(2)], axis=0)
        out[d] = both.astype(BF16)


def mix(z, matrices):
    whole = pl.BlockSpec(memory_space=pltpu.VMEM)
    return pl.pallas_call(
        mix_kernel,
        out_shape=jax.ShapeDtypeStruct((128, 80, 128), BF16),
        in_specs=[whole] * 2,
        out_specs=whole,
        scratch_shapes=[pltpu.VMEM((2, 5120, 128), F32)],
        compiler_params=pltpu.CompilerParams(vmem_limit_bytes=VMEM),
        cost_estimate=pl.CostEstimate(
            flops=16 * 4 * 640 * 512 * 128, bytes_accessed=8 << 20, transcendentals=0
        ),
        name="mix",
    )(z, matrices)


def matrix_kernel(squared, head, out):
    h = head[...]
    h = jnp.where(squared[0] == 1, h * h, h)
    high = h.astype(BF16)
    low = (h - high.astype(F32)).astype(BF16)

    def iota(shape, dim):
        return lax.broadcasted_iota(jnp.int32, shape, dim)

    down = (iota((640, 40), 0) // 16 == iota((640, 40), 1)).astype(BF16)
    along = (iota((32, 512), 1) // 16 == iota((32, 512), 0)).astype(BF16)
    same = iota((640, 512), 0) % 16 == iota((640, 512), 1) % 16
    for i, part in enumerate((high, low)):
        tall = jnp.dot(down, part, preferred_element_type=F32).astype(BF16)
        full = jnp.dot(tall, along, preferred_element_type=F32)
        out[i] = jnp.where(same, full, 0.0).astype(BF16)


def mixing_matrices(head_map):
    f = (lax.axis_index("x") * 2 + lax.axis_index("yl")) * 4 + lax.axis_index("z")
    squared = ((2 * f % 30) // 10 == 2).astype(jnp.int32).reshape(1)
    whole = pl.BlockSpec(memory_space=pltpu.VMEM)
    return pl.pallas_call(
        matrix_kernel,
        out_shape=jax.ShapeDtypeStruct((2, 640, 512), BF16),
        in_specs=[pl.BlockSpec(memory_space=pltpu.SMEM), whole],
        out_specs=whole,
        compiler_params=pltpu.CompilerParams(vmem_limit_bytes=VMEM),
        name="matrices",
    )(squared, head_map)


def depth_kernel(depth, r_ref, out_w, out_m, out_v):
    @pl.loop(0, 10)
    def _(step):
        core, pair = step // 5, step % 5
        starts = []
        for k in range(2):
            t = 2 * pair + k
            starts.append(pl.multiple_of(((t // 5) * 10 + core * 5 + t % 5) * 128, 128))
        for tensor, out in enumerate((out_w, out_m, out_v)):
            terms = []
            for yh in range(2):
                for rel in range(2):
                    src = (yh * 2 + core) * 32 + rel * 15 + tensor * 5 + pair
                    slot = 2 * yh + (rel + core) % 2
                    terms.append((slot, r_ref[src].astype(F32)))
            for j in range(5):
                total = None
                for slot, value in terms:
                    c = depth[j, slot]
                    c = c * c if tensor == 2 else c
                    total = c * value if total is None else total + c * value
                for k in range(2):
                    out[j, :, pl.ds(starts[k], 128)] = total[k * 40 : k * 40 + 40].astype(out.dtype)


def mix_depth(depth, received):
    whole = pl.BlockSpec(memory_space=pltpu.VMEM)
    return pl.pallas_call(
        depth_kernel,
        out_shape=tuple(jax.ShapeDtypeStruct((5, 40, COLS), dt) for dt in (BF16, F32, F32)),
        in_specs=[pl.BlockSpec(memory_space=pltpu.SMEM), whole],
        out_specs=(whole,) * 3,
        compiler_params=pltpu.CompilerParams(vmem_limit_bytes=VMEM),
        cost_estimate=pl.CostEstimate(flops=12 << 20, bytes_accessed=8 << 20, transcendentals=0),
        name="depth",
    )(depth, received)


def depth_matrix(layer_slot, depth_src, depth_coef):
    hits = (layer_slot[None, None, :] == depth_src[:, :, None]).astype(F32)
    return jnp.sum(depth_coef[:, :, None] * hits, axis=1)


def on_device(small_w, small_m, small_v, width_map, head_map, layer_slot, depth_src, depth_coef):
    own = jnp.concatenate([small_w, small_m.astype(BF16), small_v.astype(BF16)], axis=0)
    other = lax.ppermute(own, "core", ((0, 1), (1, 0)))
    pieces, rows = gather_width(width_map)
    z = widen(rows, own, other, pieces).reshape(32, 2, 128, 128)
    z = lax.all_to_all(z, GROUP, split_axis=0, concat_axis=0, tiled=True)
    y = mix(z, mixing_matrices(head_map))
    received = lax.all_to_all(y, AXES, split_axis=0, concat_axis=0, tiled=True)
    return mix_depth(depth_matrix(layer_slot, depth_src, depth_coef), received)


def solution(mesh):
    chips = Mesh(mesh.devices.reshape(SIZES), AXES)
    grp, fsdp = ("yh", "core"), GROUP
    return jax.shard_map(
        on_device,
        mesh=chips,
        in_specs=(
            P(grp, fsdp, None),
            P(grp, fsdp, None),
            P(grp, fsdp, None),
            P(AXES, None),
            P(),
            P(),
            P(),
            P(),
        ),
        out_specs=(P(None, AXES, None),) * 3,
        check_vma=False,
    )
```

time: 740 us -> 195 us (0.26); the launches traced: 730 us -> 194 us
  waiting for transfers between devices: 392 us -> 97.7 us
  local copies, waits for them, and re-layouts: 117 us -> 11.6 us
  matrix products: 99.6 us -> 0 us
  other arithmetic: 61.9 us -> 0.66 us
  Pallas kernels: 0 us -> 33.9 us
  blocking collectives: 0 us -> 14.6 us
  between operations: 14.5 us -> 0.82 us
  starting transfers between devices: 45.6 us -> 35.3 us
    all_gather x1 -> x0, waiting for transfers between devices: 344 us -> none  [on_device(): lax.all_gather(width_map, ('grp', 'fsdp'), axis=0, tiled=True)]
    dot_general x9 -> x0, matrix products: 99.6 us -> none  [the longest x2 58.4 us: project(): lax.dot_general(left, right, dims, precision=lax.Precision.HIGHEST, prefe...]
    ppermute x0 -> x10, waiting for transfers between devices: none -> 46.5 us  [the longest x9 46.5 us: shift(): return lax.ppermute(value, AXES, pairs)]
    mul x1 -> x0, local copies, waits for them, and re-layouts: 41.6 us -> none  [widen_panels(): z_v = project(panels_v, wide * wide, True)]
    unnamed x2 -> x0, other arithmetic: 34.3 us -> none
    pallas_call x0 -> x4, Pallas kernels: none -> 33.9 us  [the longest x1 17.1 us: widen(): pl.pallas_call(widen_kernel, out_shape=jax.ShapeDtypeStruct((UNITS, 128,...]
    mul x1 -> x0, other arithmetic: 27.5 us -> none  [widen_panels(): z_v = project(panels_v, wide * wide, True)]
    dot_general x1 -> x0, local copies, waits for them, and re-layouts: 26.5 us -> none  [project(): lax.dot_general(left, right, dims, preferred_element_type=jnp.float32)]
  transfers between devices with their start and end apart: 7 -> 12, of which waited for: 4 -> 8; matrix products, arithmetic and copies ran while one was open for 29% -> 4% of each run, Pallas kernels for 0% -> 1%
where the time goes in v1:
time: 195 us; the launch traced here: 194 us
  waiting for transfers between devices  97.7 us (50%)
  starting transfers between devices  35.3 us (18%)
  Pallas kernels  33.9 us (17%)
  blocking collectives  14.6 us (7%)
  local copies, waits for them, and re-layouts  11.6 us (6%)
    ppermute x9, waiting for transfers between devices, shift(): return lax.ppermute(value, AXES, pairs)  46.5 us
    all_to_all x1, waiting for transfers between devices, on_device(): received = lax.all_to_all(y, AXES, split_axis=0, concat_axis=0, tiled=True)  35.1 us
    pallas_call x1, Pallas kernels, widen(): pl.pallas_call(widen_kernel, out_shape=jax.ShapeDtypeStruct((UNITS, 128,...  17.1 us
    all_to_all x1, waiting for transfers between devices, on_device(): z = lax.all_to_all(z, GROUP, split_axis=0, concat_axis=0, tiled=True)  16.1 us
    all_gather x1, blocking collectives, gather_width(): block = lax.all_gather(shard, 'z', axis=0, tiled=True)  14.6 us
    all_to_all x1, starting transfers between devices, on_device(): received = lax.all_to_all(y, AXES, split_axis=0, concat_axis=0, tiled=True)  14.2 us
    ppermute x9, starting transfers between devices, shift(): return lax.ppermute(value, AXES, pairs)  12.5 us
    unnamed x24, local copies, waits for them, and re-layouts  8.47 us
  transfers between devices with their start and end apart: 12, of which 8 were waited for; matrix products, arithmetic and copies ran while one was open for 4% of the time, Pallas kernels for 1%

profile of v1, /device:TPU:1, one launch (start us, length us, event | category | flops | bytes accessed | tf_op | source)
XLA Modules:
  0.0 194.5 jit_solution(4872326101368528819)
XLA Ops:
  0.6 14.6 %all-gather = bf16[4,20,4096]{2,1,0:T(8,128)(2,1)S(1)} all-gather(bf16[1,20,4096]{2,1,0:T(8,128)(2,1)} %bitcast.20), channel_id=1, replica_groups=mesh['yh'=2,'core'=2,'x'=4,'yl'=2,'z'=4] {'z'}, dimensions={0}, use_global_device_ids=true | all-gather | bytes 819200 | tf_op jit(solution)/shard_map/all_gather | solution.py:39
  15.2 1.0 reshape.23
  16.2 2.5 %collective-permute-start.2 = (bf16[80,4096]{1,0:T(8,128)(2,1)}, bf16[80,4096]{1,0:T(8,128)(2,1)S(1)}, u32[]{:S(2)}, u32[]{:S(2)}) collective-permute-start(bf16[80,4096]{1,0:T(8,128)(2,1)} %reshape.23), channel_id=1, source_target_pairs={{0,68},{1,69},{2,70},{3,71},{4,0},{5,1},{6,2},{7,3},{8,76},{9,77},... | collective-permute-start | bytes 1966088 | tf_op jit(solution)/shard_map/ppermute | solution.py:35
  20.1 1.1 copy-done.5
  21.5 3.1 %collective-permute-start = (bf16[3,128,4096]{2,1,0:T(8,128)(2,1)S(1)}, bf16[3,128,4096]{2,1,0:T(8,128)(2,1)}, u32[]{:S(2)}, u32[]{:S(2)}) collective-permute-start(bf16[3,128,4096]{2,1,0:T(8,128)(2,1)S(1)} %pad_maximum_fusion.own), channel_id=1, source_target_pairs={{0,32},{32,0},{1,33},{33,1},{2,34},{34,2},{3,35},{35,3},{4,36},{36... | collective-permute-start | bytes 9437192 | tf_op jit(solution)/shard_map/ppermute | solution.py:250
  24.7 2.0 %constant_dynamic-update-slice_fusion.1 = bf16[160,4096]{1,0:T(8,128)(2,1)} fusion(bf16[80,4096]{1,0:T(8,128)(2,1)} %reshape.23), kind=kLoop, calls=%fused_computation.2 | loop fusion | bytes 1310720
  26.6 7.0 %collective-permute-done.2 = bf16[80,4096]{1,0:T(8,128)(2,1)S(1)} collective-permute-done((bf16[80,4096]{1,0:T(8,128)(2,1)}, bf16[80,4096]{1,0:T(8,128)(2,1)S(1)}, u32[]{:S(2)}, u32[]{:S(2)}) %collective-permute-start.2) | collective-permute-done | bytes 655392 | tf_op jit(solution)/shard_map/ppermute | solution.py:35
  33.6 0.9 constant_dynamic-update-slice_fusion.3
  34.5 0.9 constant_dynamic-update-slice_fusion.2.refs_1_
  35.3 2.7 %collective-permute-start.7 = (bf16[160,4096]{1,0:T(8,128)(2,1)}, bf16[160,4096]{1,0:T(8,128)(2,1)}, u32[]{:S(2)}, u32[]{:S(2)}) collective-permute-start(bf16[160,4096]{1,0:T(8,128)(2,1)} %constant_dynamic-update-slice_fusion.2.refs_1_), channel_id=1, source_target_pairs={{0,24},{1,25},{2,26},{3,27},{4,28},{5,29},{6,30},{7,31},{8,0},{9,1... | collective-permute-start | bytes 3932168 | tf_op jit(solution)/shard_map/ppermute | solution.py:35
  38.1 0.9 constant_dynamic-update-slice_fusion.refs_0_
  39.0 1.3 collective-permute-start.5
  40.3 1.4 collective-permute-start.6
  41.7 11.2 %collective-permute-done.7.refs_5_ = bf16[160,4096]{1,0:T(8,128)(2,1)} collective-permute-done((bf16[160,4096]{1,0:T(8,128)(2,1)}, bf16[160,4096]{1,0:T(8,128)(2,1)}, u32[]{:S(2)}, u32[]{:S(2)}) %collective-permute-start.7) | collective-permute-done | bytes 1310752 | tf_op jit(solution)/shard_map/ppermute | solution.py:35
  52.9 3.4 %collective-permute-start.9 = (bf16[160,4096]{1,0:T(8,128)(2,1)}, bf16[160,4096]{1,0:T(8,128)(2,1)}, u32[]{:S(2)}, u32[]{:S(2)}) collective-permute-start(bf16[160,4096]{1,0:T(8,128)(2,1)} %collective-permute-done.7.refs_5_), channel_id=1, source_target_pairs={{0,24},{1,25},{2,26},{3,27},{4,28},{5,29},{6,30},{7,31},{8,0},{9,1... | collective-permute-start | bytes 3932168 | tf_op jit(solution)/shard_map/ppermute | solution.py:35
  56.4 0.9 collective-permute-done.4.refs_2_
  57.2 0.7 stack.67.rows
  57.9 13.4 %collective-permute-done.5.refs_3_ = bf16[160,4096]{1,0:T(8,128)(2,1)} collective-permute-done((bf16[160,4096]{1,0:T(8,128)(2,1)}, bf16[160,4096]{1,0:T(8,128)(2,1)}, u32[]{:S(2)}, u32[]{:S(2)}) %collective-permute-start.5) | collective-permute-done | bytes 1310752 | tf_op jit(solution)/shard_map/ppermute | solution.py:35
  71.3 9.7 %collective-permute-done.9.refs_7_ = bf16[160,4096]{1,0:T(8,128)(2,1)} collective-permute-done((bf16[160,4096]{1,0:T(8,128)(2,1)}, bf16[160,4096]{1,0:T(8,128)(2,1)}, u32[]{:S(2)}, u32[]{:S(2)}) %collective-permute-start.9) | collective-permute-done | bytes 1310752 | tf_op jit(solution)/shard_map/ppermute | solution.py:35
  81.0 4.3 %collective-permute-done.8.refs_6_ = bf16[160,4096]{1,0:T(8,128)(2,1)} collective-permute-done((bf16[160,4096]{1,0:T(8,128)(2,1)}, bf16[160,4096]{1,0:T(8,128)(2,1)}, u32[]{:S(2)}, u32[]{:S(2)}) %collective-permute-start.8) | collective-permute-done | bytes 1310752 | tf_op jit(solution)/shard_map/ppermute | solution.py:35
  85.3 17.1 %widen.1 = bf16[64,128,128]{2,1,0:T(8,128)(2,1)} custom-call(s32[16]{0:T(128)} %stack.67.rows, bf16[3,128,4096]{2,1,0:T(8,128)(2,1)} %copy-done.1, bf16[3,128,4096]{2,1,0:T(8,128)(2,1)} %collective-permute-done.other, bf16[160,4096]{1,0:T(8,128)(2,1)} %constant_dynamic-update-slice_fusion.refs_0_, ...), custom_call_target="tpu_custom_call" | custom-call | flops 8053063680 | bytes 20971520 | tf_op jit(solution)/shard_map/widen/pallas_call | solution.py:114
  102.5 5.6 %all-to-all-start = ((bf16[32,2,128,128]{3,2,1,0:T(8,128)(2,1)}), bf16[32,2,128,128]{3,2,1,0:T(8,128)(2,1)S(1)}, u32[]{:S(2)}, u32[]{:S(2)}) async-start(bf16[32,2,128,128]{3,2,1,0:T(8,128)(2,1)} %bitcast.19), calls=%async_computation | async-start | bytes 4194304 | tf_op jit(solution)/shard_map/all_to_all | solution.py:253
  108.1 0.7 copy.20.head
  108.8 2.5 %matrices.1.m_ref = bf16[2,640,512]{2,1,0:T(8,128)(2,1)} custom-call(s32[1]{0:T(128)} %bitcast.18.squared, f32[40,32]{1,0:T(8,128)} %copy.20.head), custom_call_target="tpu_custom_call" | custom-call | tf_op jit(solution)/shard_map/matrices/pallas_call | solution.py:195
  111.3 16.1 %all-to-all-done.z_ref = bf16[32,2,128,128]{3,2,1,0:T(8,128)(2,1)S(1)} async-done(((bf16[32,2,128,128]{3,2,1,0:T(8,128)(2,1)}), bf16[32,2,128,128]{3,2,1,0:T(8,128)(2,1)S(1)}, u32[]{:S(2)}, u32[]{:S(2)}) %all-to-all-start) | async-done | bytes 2097184 | tf_op jit(solution)/shard_map/all_to_all | solution.py:253
  127.4 1.3 copy-done.4
  128.8 7.9 %mix.1 = bf16[128,80,128]{2,1,0:T(8,128)(2,1)} custom-call(bf16[32,2,128,128]{3,2,1,0:T(8,128)(2,1)} %copy-done.4, bf16[2,640,512]{2,1,0:T(8,128)(2,1)} %matrices.1.m_ref), custom_call_target="tpu_custom_call" | custom-call | flops 2684354560 | bytes 8388608 | tf_op jit(solution)/shard_map/mix/pallas_call | solution.py:159
  136.7 14.2 %all-to-all-start.1 = ((bf16[128,80,128]{2,1,0:T(8,128)(2,1)}), bf16[128,80,128]{2,1,0:T(8,128)(2,1)S(1)}, u32[]{:S(2)}, u32[]{:S(2)}) async-start(bf16[128,80,128]{2,1,0:T(8,128)(2,1)} %mix.1), calls=%async_computation.1 | async-start | bytes 5242880 | tf_op jit(solution)/shard_map/all_to_all | solution.py:255
  150.9 0.7 copy.21.depth
  151.6 35.1 %all-to-all-done.1.r_ref = bf16[128,80,128]{2,1,0:T(8,128)(2,1)S(1)} async-done(((bf16[128,80,128]{2,1,0:T(8,128)(2,1)}), bf16[128,80,128]{2,1,0:T(8,128)(2,1)S(1)}, u32[]{:S(2)}, u32[]{:S(2)}) %all-to-all-start.1) | async-done | bytes 2621472 | tf_op jit(solution)/shard_map/all_to_all | solution.py:255
  186.7 1.5 copy-done
  188.2 6.3 %depth.1 = (bf16[5,40,2560]{2,1,0:T(8,128)(2,1)}, f32[5,40,2560]{2,1,0:T(8,128)}, f32[5,40,2560]{2,1,0:T(8,128)}) custom-call(f32[5,4]{1,0:T(8,128)} %copy.21.depth, bf16[128,80,128]{2,1,0:T(8,128)(2,1)} %copy-done), custom_call_target="tpu_custom_call" | custom-call | flops 12582912 | bytes 8388608 | tf_op jit(solution)/shard_map/depth/pallas_call | solution.py:232
  (29 shorter events, 1.9 us)
Async XLA Ops:
  0.6 19.2 %copy-start.2 = (f32[1,128,4096]{2,1,0:T(8,128)S(1)}, f32[1,128,4096]{2,1,0:T(8,128)}, u32[]{:S(2)}) copy-start(f32[1,128,4096]{2,1,0:T(8,128)} %param.9) | copy-start | bytes 6291460
  16.2 3.7 %copy-start.3 = (f32[1,128,4096]{2,1,0:T(8,128)S(1)}, f32[1,128,4096]{2,1,0:T(8,128)}, u32[]{:S(2)}) copy-start(f32[1,128,4096]{2,1,0:T(8,128)} %param.10) | copy-start | bytes 6291460
  16.2 17.4 %collective-permute-start.2 = (bf16[80,4096]{1,0:T(8,128)(2,1)}, bf16[80,4096]{1,0:T(8,128)(2,1)S(1)}, u32[]{:S(2)}, u32[]{:S(2)}) collective-permute-start(bf16[80,4096]{1,0:T(8,128)(2,1)} %reshape.23), channel_id=1, source_target_pairs={{0,68},{1,69},{2,70},{3,71},{4,0},{5,1},{6,2},{7,3},{8,76},{9,77},... | collective-permute-start | bytes 1966088 | tf_op jit(solution)/shard_map/ppermute | solution.py:35
  18.7 15.8 %collective-permute-start.3 = (bf16[80,4096]{1,0:T(8,128)(2,1)}, bf16[80,4096]{1,0:T(8,128)(2,1)S(1)}, u32[]{:S(2)}, u32[]{:S(2)}) collective-permute-start(bf16[80,4096]{1,0:T(8,128)(2,1)} %reshape.23), channel_id=1, source_target_pairs={{0,64},{1,65},{2,66},{3,67},{4,68},{5,69},{6,70},{7,71},{8,72},{9,... | collective-permute-start | bytes 1966088 | tf_op jit(solution)/shard_map/ppermute | solution.py:35
  19.2 18.9 %collective-permute-start.1 = (bf16[80,4096]{1,0:T(8,128)(2,1)}, bf16[80,4096]{1,0:T(8,128)(2,1)S(1)}, u32[]{:S(2)}, u32[]{:S(2)}) collective-permute-start(bf16[80,4096]{1,0:T(8,128)(2,1)} %reshape.23), channel_id=1, source_target_pairs={{0,4},{1,5},{2,6},{3,7},{4,64},{5,65},{6,66},{7,67},{8,12},{9,13},... | collective-permute-start | bytes 1966088 | tf_op jit(solution)/shard_map/ppermute | solution.py:35
  19.9 1.2 copy-start.5
  21.5 63.8 %copy-start.1 = (bf16[3,128,4096]{2,1,0:T(8,128)(2,1)}, bf16[3,128,4096]{2,1,0:T(8,128)(2,1)S(1)}, u32[]{:S(2)}) copy-start(bf16[3,128,4096]{2,1,0:T(8,128)(2,1)S(1)} %pad_maximum_fusion.own) | copy-start | bytes 9437188
  21.5 49.8 %collective-permute-start = (bf16[3,128,4096]{2,1,0:T(8,128)(2,1)S(1)}, bf16[3,128,4096]{2,1,0:T(8,128)(2,1)}, u32[]{:S(2)}, u32[]{:S(2)}) collective-permute-start(bf16[3,128,4096]{2,1,0:T(8,128)(2,1)S(1)} %pad_maximum_fusion.own), channel_id=1, source_target_pairs={{0,32},{32,0},{1,33},{33,1},{2,34},{34,2},{3,35},{35,3},{4,36},{36... | collective-permute-start | bytes 9437192 | tf_op jit(solution)/shard_map/ppermute | solution.py:250
  35.3 17.6 %collective-permute-start.7 = (bf16[160,4096]{1,0:T(8,128)(2,1)}, bf16[160,4096]{1,0:T(8,128)(2,1)}, u32[]{:S(2)}, u32[]{:S(2)}) collective-permute-start(bf16[160,4096]{1,0:T(8,128)(2,1)} %constant_dynamic-update-slice_fusion.2.refs_1_), channel_id=1, source_target_pairs={{0,24},{1,25},{2,26},{3,27},{4,28},{5,29},{6,30},{7,31},{8,0},{9,1... | collective-permute-start | bytes 3932168 | tf_op jit(solution)/shard_map/ppermute | solution.py:35
  39.0 18.3 %collective-permute-start.4 = (bf16[160,4096]{1,0:T(8,128)(2,1)}, bf16[160,4096]{1,0:T(8,128)(2,1)}, u32[]{:S(2)}, u32[]{:S(2)}) collective-permute-start(bf16[160,4096]{1,0:T(8,128)(2,1)} %constant_dynamic-update-slice_fusion.refs_0_), channel_id=1, source_target_pairs={{0,8},{1,9},{2,10},{3,11},{4,12},{5,13},{6,14},{7,15},{8,16},{9,17... | collective-permute-start | bytes 3932168 | tf_op jit(solution)/shard_map/ppermute | solution.py:35
  39.0 32.3 %collective-permute-start.5 = (bf16[160,4096]{1,0:T(8,128)(2,1)}, bf16[160,4096]{1,0:T(8,128)(2,1)}, u32[]{:S(2)}, u32[]{:S(2)}) collective-permute-start(bf16[160,4096]{1,0:T(8,128)(2,1)} %constant_dynamic-update-slice_fusion.2.refs_1_), channel_id=1, source_target_pairs={{0,8},{1,9},{2,10},{3,11},{4,12},{5,13},{6,14},{7,15},{8,16},{9,17... | collective-permute-start | bytes 3932168 | tf_op jit(solution)/shard_map/ppermute | solution.py:35
  40.3 31.0 %collective-permute-start.6 = (bf16[160,4096]{1,0:T(8,128)(2,1)}, bf16[160,4096]{1,0:T(8,128)(2,1)}, u32[]{:S(2)}, u32[]{:S(2)}) collective-permute-start(bf16[160,4096]{1,0:T(8,128)(2,1)} %constant_dynamic-update-slice_fusion.refs_0_), channel_id=1, source_target_pairs={{0,24},{1,25},{2,26},{3,27},{4,28},{5,29},{6,30},{7,31},{8,0},{9,1... | collective-permute-start | bytes 3932168 | tf_op jit(solution)/shard_map/ppermute | solution.py:35
  52.9 28.1 %collective-permute-start.9 = (bf16[160,4096]{1,0:T(8,128)(2,1)}, bf16[160,4096]{1,0:T(8,128)(2,1)}, u32[]{:S(2)}, u32[]{:S(2)}) collective-permute-start(bf16[160,4096]{1,0:T(8,128)(2,1)} %collective-permute-done.7.refs_5_), channel_id=1, source_target_pairs={{0,24},{1,25},{2,26},{3,27},{4,28},{5,29},{6,30},{7,31},{8,0},{9,1... | collective-permute-start | bytes 3932168 | tf_op jit(solution)/shard_map/ppermute | solution.py:35
  57.2 28.1 %collective-permute-start.8 = (bf16[160,4096]{1,0:T(8,128)(2,1)}, bf16[160,4096]{1,0:T(8,128)(2,1)}, u32[]{:S(2)}, u32[]{:S(2)}) collective-permute-start(bf16[160,4096]{1,0:T(8,128)(2,1)} %collective-permute-done.4.refs_2_), channel_id=1, source_target_pairs={{0,8},{1,9},{2,10},{3,11},{4,12},{5,13},{6,14},{7,15},{8,16},{9,17... | collective-permute-start | bytes 3932168 | tf_op jit(solution)/shard_map/ppermute | solution.py:35
  102.5 5.6 %copy-start.6 = (f32[40,32]{0,1:T(8,128)S(1)}, f32[40,32]{0,1:T(8,128)}, u32[]{:S(2)}) copy-start(f32[40,32]{0,1:T(8,128)} %param.12) | copy-start | bytes 15364
  102.5 24.9 %all-to-all-start = ((bf16[32,2,128,128]{3,2,1,0:T(8,128)(2,1)}), bf16[32,2,128,128]{3,2,1,0:T(8,128)(2,1)S(1)}, u32[]{:S(2)}, u32[]{:S(2)}) async-start(bf16[32,2,128,128]{3,2,1,0:T(8,128)(2,1)} %bitcast.19), calls=%async_computation | async-start | bytes 4194304 | tf_op jit(solution)/shard_map/all_to_all | solution.py:253
  127.4 1.3 copy-start.4
  136.7 14.2 %copy-start.7 = (f32[5,2]{0,1:T(2,128)S(1)}, f32[5,2]{0,1:T(2,128)}, u32[]{:S(2)}) copy-start(f32[5,2]{0,1:T(2,128)} %param.15) | copy-start | bytes 124
  136.7 14.2 %copy-start.8 = (s32[5,2]{0,1:T(2,128)S(1)}, s32[5,2]{0,1:T(2,128)}, u32[]{:S(2)}) copy-start(s32[5,2]{0,1:T(2,128)} %param.14) | copy-start | bytes 124
  136.7 14.2 %copy-start.9 = (s32[4]{0:T(128)S(1)}, s32[4]{0:T(128)}, u32[]{:S(2)}) copy-start(s32[4]{0:T(128)} %param.13) | copy-start | bytes 52
  136.7 50.0 %all-to-all-start.1 = ((bf16[128,80,128]{2,1,0:T(8,128)(2,1)}), bf16[128,80,128]{2,1,0:T(8,128)(2,1)S(1)}, u32[]{:S(2)}, u32[]{:S(2)}) async-start(bf16[128,80,128]{2,1,0:T(8,128)(2,1)} %mix.1), calls=%async_computation.1 | async-start | bytes 5242880 | tf_op jit(solution)/shard_map/all_to_all | solution.py:255
  186.7 1.5 copy-start

commit v2 on v1

v2 whole, which is shorter than its diff:
```python
import jax
import jax.numpy as jnp
from jax import lax
from jax.experimental import pallas as pl
from jax.experimental.pallas import tpu as pltpu
from jax.sharding import Mesh, PartitionSpec as P

SIZES = (2, 2, 4, 2, 4)
AXES = ("yh", "core", "x", "yl", "z")
GROUP = ("x", "yl", "z")
BF16, F32 = jnp.bfloat16, jnp.float32

COLS, HALF, DEPTH = 2560, 1280, 4096
BLOCK = 80
UNITS = 64
VMEM = 26 * 1024 * 1024


def place(yh, core, x, yl, z):
    return (((yh * 2 + core) * 4 + x) * 2 + yl) * 4 + z


def shift(value, axis_of_core, by):
    pairs = []
    for yh in range(2):
        for core in range(2):
            for x in range(4):
                for yl in range(2):
                    for z in range(4):
                        to = [x, 2 * yh + yl]
                        to[axis_of_core[core]] = (to[axis_of_core[core]] + by) % 4
                        pairs.append(
                            (place(yh, core, x, yl, z), place(to[1] // 2, core, to[0], to[1] % 2, z))
                        )
    return lax.ppermute(value, AXES, pairs)


def order_kernel(mine, own, before, after, across, out, wide, block, sem):
    for at in range(4):
        for by, shard in ((0, own), (1, after), (2, across), (3, before)):

            @pl.when((at - mine[0] + 4) % 4 == by)
            def _():
                wide[20 * at : 20 * at + 20, :] = shard[...].astype(F32)

    block[...] = wide[...].astype(BF16)
    copy = pltpu.make_async_copy(block, out, sem)
    copy.start()
    copy.wait()


def in_order(mine, *shards):
    whole = pl.BlockSpec(memory_space=pltpu.VMEM)
    return pl.pallas_call(
        order_kernel,
        out_shape=jax.ShapeDtypeStruct((BLOCK, DEPTH), BF16),
        in_specs=[pl.BlockSpec(memory_space=pltpu.SMEM)] + [whole] * 4,
        out_specs=pl.BlockSpec(memory_space=pltpu.HBM),
        scratch_shapes=[
            pltpu.VMEM((BLOCK, DEPTH), F32),
            pltpu.VMEM((BLOCK, DEPTH), BF16),
            pltpu.SemaphoreType.DMA,
        ],
        compiler_params=pltpu.CompilerParams(vmem_limit_bytes=VMEM),
        name="order",
    )(mine, *shards)


def once(value, *done):
    return lax.optimization_barrier((value, *done))[0]


def grow_width(shard, small_w, small_m, small_v):
    core, z = lax.axis_index("core"), lax.axis_index("z")
    x = lax.axis_index("x")
    y = lax.axis_index("yh") * 2 + lax.axis_index("yl")
    q, p = jnp.where(core == 0, x, y), jnp.where(core == 0, y, x)

    def along_p(value, by):
        return shift(value, (1, 0), by)

    def along_q(value, by):
        return shift(value, (0, 1), by)

    def along_z(value, by):
        return lax.ppermute(value, "z", [(i, (i + by) % 4) for i in range(4)])

    before, after, across = along_p(shard, 1), along_p(shard, -1), along_p(shard, 2)
    own = jnp.concatenate([small_w, small_m.astype(BF16), small_v.astype(BF16)], axis=0)
    other = lax.ppermute(own, "core", ((0, 1), (1, 0)))
    a = in_order(p.reshape(1), shard, before, after, across)
    a_before, a_after = along_q(a, 1), along_q(a, -1)
    b_before, b_after = along_z(a, 1), along_z(a, -1)
    a_across = along_q(a_before, 1)
    b = once(jnp.concatenate([b_before, b_after], axis=0), a_across, a_after, other)
    d = along_z(once(a, b_before), 2)
    b_before, b_after = along_q(b, 1), along_q(b, -1)
    here = jnp.stack([core, q, z]).astype(jnp.int32)
    first = (
        (a, b, a_before, a_after, a_across),
        ((0, 0), (0, -1), (0, 1), (-1, 0), (1, 0), (2, 0)),
    )
    z_first = widen(own, other, first)
    d_sent = once(d, z_first)
    d_before, d_after = along_q(d_sent, 1), along_q(d_sent, -1)
    second = ((d, b_before, b_after), ((0, 2), (-1, -1), (-1, 1), (1, -1), (1, 1)))
    b_across = along_q(b_after, -1)
    z_second = widen(own, other, second)
    d_across = along_q(once(d_before, z_second), 1)
    last = (
        (b_across, d_before, d_after, d_across),
        ((2, -1), (2, 1), (-1, 2), (1, 2), (2, 2)),
    )
    partial = spread((first[1], second[1]), (z_first, z_second), here)
    return widen_last(own, other, last, partial, here)


def load_and_project(own, other, pieces, b_ref, a_ref, b_sem, a_sem):
    copies = []
    row = 0
    for i, piece in enumerate(pieces):
        rows = piece.shape[0]
        copies.append(pltpu.make_async_copy(piece, b_ref.at[pl.ds(row, rows)], b_sem.at[i]))
        row += rows
    for i, (src, dst) in enumerate(
        (
            (own.at[0:2], a_ref.at[0:2]),
            (other.at[0:2], a_ref.at[2:4]),
            (own.at[2:3], a_ref.at[4:5]),
            (other.at[2:3], a_ref.at[5:6]),
        )
    ):
        copies.append(pltpu.make_async_copy(src, dst, a_sem.at[i]))
    for copy in copies:
        copy.start()
    for copy in copies:
        copy.wait()
    nt = (((1,), (1,)), ((), ()))
    b = b_ref[...]
    wm = lax.dot_general(a_ref[0:4].reshape(512, DEPTH), b, nt, preferred_element_type=F32)
    v = lax.dot_general(a_ref[4:6].reshape(256, DEPTH), b * b, nt, preferred_element_type=F32)
    return wm.astype(BF16), v.astype(BF16)


def widen_kernel(n, own, other, *refs):
    wm, v = load_and_project(own, other, refs[:n], *refs[n + 1 :])
    refs[n][0:512] = wm
    refs[n][512:768] = v


def spread_columns(places, values, here, previous, out):
    core, q, z = here[0], here[1], here[2]
    row = lax.broadcasted_iota(jnp.int32, (BLOCK, 256), 0)
    lane = lax.broadcasted_iota(jnp.int32, (BLOCK, 256), 1)
    third = [(row >= 20 * k).astype(jnp.int32) for k in (1, 2, 3)]
    line = third[0] + third[1] + third[2]
    inner = row - 20 * line
    spot = (
        inner
        + jnp.where(core == 0, third[1] * 640 + (line - 2 * third[1]) * 80, line * 160)
        - lane
    )

    @pl.loop(0, HALF // 256)
    def _(tile):
        total = None
        for group, value in zip(places, values):
            ones = []
            for dq, dz in group:
                bq, bz = lax.rem(q + dq + 4, 4), lax.rem(z + dz + 4, 4)
                base = bz * 20 + jnp.where(
                    core == 0, bq * 160, (bq // 2) * 640 + lax.rem(bq, 2) * 80
                )
                ones.append(jnp.where(spot == tile * 256 - base, 1.0, 0.0).astype(BF16))
            moved = jnp.dot(
                value[...], jnp.concatenate(ones, axis=0), preferred_element_type=F32
            )
            total = moved if total is None else total + moved
        total = total.astype(BF16)
        for first, at in ((0, 0), (10, 1), (20, 4), (30, 2), (40, 3), (50, 5)):
            for half in range(2):
                t = first + tile * 2 + half
                part = total[at * 128 : at * 128 + 128, half * 128 : half * 128 + 128]
                out[t] = part if previous is None else previous[t] + part

    out[60:64] = jnp.zeros((4, 128, 128), BF16)


def spread(places, values, here):
    def kernel(here, *refs):
        spread_columns(places, refs[:-1], here, None, refs[-1])

    whole = pl.BlockSpec(memory_space=pltpu.VMEM)
    rows = BLOCK * sum(len(group) for group in places)
    return pl.pallas_call(
        kernel,
        out_shape=jax.ShapeDtypeStruct((UNITS, 128, 128), BF16),
        in_specs=[pl.BlockSpec(memory_space=pltpu.SMEM)] + [whole] * len(values),
        out_specs=whole,
        compiler_params=pltpu.CompilerParams(vmem_limit_bytes=VMEM),
        cost_estimate=pl.CostEstimate(
            flops=2 * 768 * rows * HALF, bytes_accessed=4 << 20, transcendentals=0
        ),
        name="spread",
    )(here, *values)


def last_kernel(n, places, here, own, other, *refs):
    last = refs[-1]
    wm, v = load_and_project(own, other, refs[:n], *refs[n + 2 : -1])
    last[0:512] = wm
    last[512:768] = v
    spread_columns([places], [last], here, refs[n], refs[n + 1])


def project_call(kernel, operands, specs, out, rows, n, more_scratch, flops, name):
    return pl.pallas_call(
        kernel,
        out_shape=jax.ShapeDtypeStruct(out, BF16),
        in_specs=specs,
        out_specs=pl.BlockSpec(memory_space=pltpu.VMEM),
        scratch_shapes=[
            pltpu.VMEM((rows, DEPTH), BF16),
            pltpu.VMEM((6, 128, DEPTH), BF16),
            pltpu.SemaphoreType.DMA((n,)),
            pltpu.SemaphoreType.DMA((4,)),
            *more_scratch,
        ],
        compiler_params=pltpu.CompilerParams(vmem_limit_bytes=VMEM),
        cost_estimate=pl.CostEstimate(
            flops=2 * 768 * rows * DEPTH + flops, bytes_accessed=10 << 20, transcendentals=0
        ),
        name=name,
    )(*operands)


def widen(own, other, group):
    pieces, places = group
    n, rows = len(pieces), len(places) * BLOCK

    def kernel(*refs):
        widen_kernel(n, *refs)

    return project_call(
        kernel,
        (own, other, *pieces),
        [pl.BlockSpec(memory_space=pl.ANY)] * (2 + n),
        (768, rows),
        rows,
        n,
        (),
        0,
        "widen",
    )


def widen_last(own, other, group, partial, here):
    pieces, places = group
    n, rows = len(pieces), len(places) * BLOCK

    def kernel(*refs):
        last_kernel(n, places, *refs)

    whole = pl.BlockSpec(memory_space=pltpu.VMEM)
    return project_call(
        kernel,
        (here, own, other, *pieces, partial),
        [pl.BlockSpec(memory_space=pltpu.SMEM)] + [pl.BlockSpec(memory_space=pl.ANY)] * (2 + n) + [whole],
        (UNITS, 128, 128),
        rows,
        n,
        (pltpu.VMEM((768, rows), BF16),),
        2 * 768 * HALF * rows,
        "widen_last",
    )


def mix_kernel(z_ref, m_ref, out, y_ref):
    row = pl.multiple_of(pl.program_id(0) * 32, 32)
    for k in range(2):
        block = jnp.concatenate(
            [z_ref[:, k, pl.ds(row + 16 * i, 16), :].reshape(512, 128) for i in range(2)], axis=1
        )
        y = jnp.dot(m_ref[0], block, preferred_element_type=F32)
        y = y + jnp.dot(m_ref[1], block, preferred_element_type=F32)
        for g in range(40):
            for i in range(2):
                y_ref[k, pl.ds(g * 128 + row + 16 * i, 16), :] = y[
                    g * 16 : g * 16 + 16, i * 128 : i * 128 + 128
                ]

    @pl.when(pl.program_id(0) == 3)
    def _():
        @pl.loop(0, 128, unroll=8)
        def _(d):
            first = pl.multiple_of(d * 40, 8)
            both = jnp.concatenate([y_ref[k, pl.ds(first, 40), :] for k in range(2)], axis=0)
            out[d] = both.astype(BF16)


def mix(z, matrices):
    return pl.pallas_call(
        mix_kernel,
        out_shape=jax.ShapeDtypeStruct((128, 80, 128), BF16),
        grid=(4,),
        in_specs=[
            pl.BlockSpec(memory_space=pltpu.VMEM),
            pl.BlockSpec(memory_space=pltpu.VMEM),
        ],
        out_specs=pl.BlockSpec(memory_space=pltpu.VMEM),
        scratch_shapes=[pltpu.VMEM((2, 5120, 128), F32)],
        compiler_params=pltpu.CompilerParams(vmem_limit_bytes=VMEM),
        cost_estimate=pl.CostEstimate(
            flops=16 * 4 * 640 * 512 * 128, bytes_accessed=8 << 20, transcendentals=0
        ),
        name="mix",
    )(z, matrices)


def matrix_kernel(squared, head, out):
    h = head[...]
    h = jnp.where(squared[0] == 1, h * h, h)
    high = h.astype(BF16)
    low = (h - high.astype(F32)).astype(BF16)

    def iota(shape, dim):
        return lax.broadcasted_iota(jnp.int32, shape, dim)

    down = (iota((640, 40), 0) // 16 == iota((640, 40), 1)).astype(BF16)
    along = (iota((32, 512), 1) // 16 == iota((32, 512), 0)).astype(BF16)
    same = iota((640, 512), 0) % 16 == iota((640, 512), 1) % 16
    for i, part in enumerate((high, low)):
        tall = jnp.dot(down, part, preferred_element_type=F32).astype(BF16)
        full = jnp.dot(tall, along, preferred_element_type=F32)
        out[i] = jnp.where(same, full, 0.0).astype(BF16)


def mixing_matrices(head_map):
    f = (lax.axis_index("x") * 2 + lax.axis_index("yl")) * 4 + lax.axis_index("z")
    squared = ((2 * f % 30) // 10 == 2).astype(jnp.int32).reshape(1)
    whole = pl.BlockSpec(memory_space=pltpu.VMEM)
    return pl.pallas_call(
        matrix_kernel,
        out_shape=jax.ShapeDtypeStruct((2, 640, 512), BF16),
        in_specs=[pl.BlockSpec(memory_space=pltpu.SMEM), whole],
        out_specs=whole,
        compiler_params=pltpu.CompilerParams(vmem_limit_bytes=VMEM),
        name="matrices",
    )(squared, head_map)


def depth_kernel(depth, r_ref, out_w, out_m, out_v):
    core = pl.program_id(0)
    for y_half in range(2):

        @pl.when(pl.program_id(1) == y_half)
        def _():
            for i in range(5):
                pair, k = divmod(y_half * 5 + i, 2)
                for tensor, out in enumerate((out_w, out_m, out_v)):
                    values = [
                        r_ref[yh, core, rel * 15 + tensor * 5 + pair].astype(F32)[k * 40 : k * 40 + 40]
                        for yh in range(2)
                        for rel in range(2)
                    ]
                    for j in range(5):
                        total = None
                        for n, value in enumerate(values):
                            yh, rel = divmod(n, 2)
                            c = depth[j, 2 * yh + lax.rem(rel + core, 2)]
                            c = c * c if tensor == 2 else c
                            total = c * value if total is None else total + c * value
                        out[j, :, i * 128 : i * 128 + 128] = total.astype(out.dtype)


def mix_depth(depth, received):
    block = pl.BlockSpec((5, 40, 640), lambda core, y_half: (0, 0, 2 * y_half + core))
    return pl.pallas_call(
        depth_kernel,
        out_shape=tuple(jax.ShapeDtypeStruct((5, 40, COLS), dt) for dt in (BF16, F32, F32)),
        grid=(2, 2),
        in_specs=[
            pl.BlockSpec(memory_space=pltpu.SMEM),
            pl.BlockSpec(memory_space=pltpu.VMEM),
        ],
        out_specs=(block,) * 3,
        compiler_params=pltpu.CompilerParams(vmem_limit_bytes=VMEM),
        cost_estimate=pl.CostEstimate(flops=12 << 20, bytes_accessed=8 << 20, transcendentals=0),
        name="depth",
    )(depth, received.reshape(2, 2, 32, 80, 128))


def depth_matrix(layer_slot, depth_src, depth_coef):
    hits = (layer_slot[None, None, :] == depth_src[:, :, None]).astype(F32)
    return jnp.sum(depth_coef[:, :, None] * hits, axis=1)


def on_device(small_w, small_m, small_v, width_map, head_map, layer_slot, depth_src, depth_coef):
    z = grow_width(width_map, small_w, small_m, small_v)
    z = z.reshape(32, 2, 128, 128)
    z = lax.all_to_all(z, GROUP, split_axis=0, concat_axis=0, tiled=True)
    y = mix(z, mixing_matrices(head_map))
    received = lax.all_to_all(y, AXES, split_axis=0, concat_axis=0, tiled=True)
    return mix_depth(depth_matrix(layer_slot, depth_src, depth_coef), received)


def solution(mesh):
    chips = Mesh(mesh.devices.reshape(SIZES), AXES)
    grp, fsdp = ("yh", "core"), GROUP
    return jax.shard_map(
        on_device,
        mesh=chips,
        in_specs=(
            P(grp, fsdp, None),
            P(grp, fsdp, None),
            P(grp, fsdp, None),
            P(AXES, None),
            P(),
            P(),
            P(),
            P(),
        ),
        out_specs=(P(None, AXES, None),) * 3,
        check_vma=False,
    )
```

time: 195 us -> 183 us (0.938)
  blocking collectives: 14.6 us -> 0 us
  waiting for transfers between devices: 97.7 us -> 86.9 us
  starting transfers between devices: 35.3 us -> 44.4 us
  Pallas kernels: 33.9 us -> 36.6 us
    ppermute x9 -> x12, waiting for transfers between devices: 46.5 us -> 23.4 us  [shift(): return lax.ppermute(value, AXES, pairs)]
    all_gather x1 -> x0, blocking collectives: 14.6 us -> none  [gather_width(): block = lax.all_gather(shard, 'z', axis=0, tiled=True)]
    ppermute x1 -> x4, waiting for transfers between devices: 0.01 us -> 10.4 us  [the longest x3 10.4 us: along_z(): return lax.ppermute(value, 'z', [(i, (i + by) % 4) for i in range(4)])]
    pallas_call x1 -> x5, Pallas kernels: 17.1 us -> 26.4 us  [the longest x3 21.3 us: project_call(): pl.pallas_call(kernel, out_shape=jax.ShapeDtypeStruct(out, BF16), in_spec...]
    ppermute x1 -> x4, starting transfers between devices: 3.14 us -> 8.86 us  [the longest x3 7.36 us: along_z(): return lax.ppermute(value, 'z', [(i, (i + by) % 4) for i in range(4)])]
    all_to_all x1, starting transfers between devices: 14.2 us -> 17.7 us  [on_device(): received = lax.all_to_all(y, AXES, split_axis=0, concat_axis=0, tiled=True)]
    pallas_call x1, Pallas kernels: 7.88 us -> 5.33 us  [mix(): pl.pallas_call(mix_kernel, out_shape=jax.ShapeDtypeStruct((128, 80, 128),...]
    unnamed x24 -> x31, local copies, waits for them, and re-layouts: 8.47 us -> 10.7 us
  transfers between devices with their start and end apart: 12 -> 18, of which waited for: 8 -> 12; matrix products, arithmetic and copies ran while one was open for 4% -> 0% of each run, Pallas kernels for 1% -> 10%
where the time goes in v2:
time: 183 us; the launch traced here: 182 us
  waiting for transfers between devices  86.9 us (47%)
  starting transfers between devices  44.4 us (24%)
  Pallas kernels  36.6 us (20%)
  local copies, waits for them, and re-layouts  10.8 us (6%)
  other arithmetic  2.59 us (1%)
    all_to_all x1, waiting for transfers between devices, on_device(): received = lax.all_to_all(y, AXES, split_axis=0, concat_axis=0, tiled=True)  35.5 us
    ppermute x12, waiting for transfers between devices, shift(): return lax.ppermute(value, AXES, pairs)  23.4 us
    pallas_call x3, Pallas kernels, project_call(): pl.pallas_call(kernel, out_shape=jax.ShapeDtypeStruct(out, BF16), in_spec...  21.3 us
    all_to_all x1, starting transfers between devices, on_device(): received = lax.all_to_all(y, AXES, split_axis=0, concat_axis=0, tiled=True)  17.7 us
    all_to_all x1, waiting for transfers between devices, on_device(): z = lax.all_to_all(z, GROUP, split_axis=0, concat_axis=0, tiled=True)  17.6 us
    ppermute x12, starting transfers between devices, shift(): return lax.ppermute(value, AXES, pairs)  11 us
    unnamed x31, local copies, waits for them, and re-layouts  10.7 us
    ppermute x3, waiting for transfers between devices, along_z(): return lax.ppermute(value, 'z', [(i, (i + by) % 4) for i in range(4)])  10.4 us
  transfers between devices with their start and end apart: 18, of which 12 were waited for; matrix products, arithmetic and copies ran while one was open for 0% of the time, Pallas kernels for 10%

profile of v2, /device:TPU:1, one launch (start us, length us, event | category | flops | bytes accessed | tf_op | source)
XLA Modules:
  0.0 182.2 jit_solution(2416549885914387252)
XLA Ops:
  0.6 1.9 %convert_element_type.8 = bf16[1,128,4096]{2,1,0:T(8,128)(2,1)S(1)} convert(f32[1,128,4096]{2,1,0:T(8,128)} %param.9) | non-fusion elementwise | flops 524288 | bytes 3145728 | tf_op jit(solution)/shard_map/convert_element_type | solution.py:89
  4.4 1.5 collective-permute-start
  5.9 1.3 collective-permute-start.1
  7.2 1.4 collective-permute-start.2
  8.6 1.6 collective-permute-start.3
  10.2 1.7 collective-permute-done.1.before
  12.1 3.1 %collective-permute-done.3.across = bf16[20,4096]{1,0:T(8,128)(2,1)} collective-permute-done((bf16[20,4096]{1,0:T(8,128)(2,1)S(1)}, bf16[20,4096]{1,0:T(8,128)(2,1)}, u32[]{:S(2)}, u32[]{:S(2)}) %collective-permute-start.3) | collective-permute-done | bytes 163872 | tf_op jit(solution)/shard_map/ppermute | solution.py:35
  15.2 1.6 order.1.refs_2_
  17.9 1.6 collective-permute-start.4
  19.6 2.1 %collective-permute-start.5 = (bf16[80,4096]{1,0:T(8,128)(2,1)S(1)}, bf16[80,4096]{1,0:T(8,128)(2,1)S(1)}, u32[]{:S(2)}, u32[]{:S(2)}) collective-permute-start(bf16[80,4096]{1,0:T(8,128)(2,1)S(1)} %order.1.refs_2_), channel_id=1, source_target_pairs={{0,3},{1,0},{2,1},{3,2},{4,7},{5,4},{6,5},{7,6},{8,11},{9,8},{10,9... | collective-permute-start | bytes 1966088 | tf_op jit(solution)/shard_map/ppermute | solution.py:86
  21.7 1.9 %collective-permute-start.8 = (bf16[80,4096]{1,0:T(8,128)(2,1)S(1)}, bf16[80,4096]{1,0:T(8,128)(2,1)S(1)}, u32[]{:S(2)}, u32[]{:S(2)}) collective-permute-start(bf16[80,4096]{1,0:T(8,128)(2,1)S(1)} %order.1.refs_2_), channel_id=1, source_target_pairs={{0,24},{1,25},{2,26},{3,27},{4,28},{5,29},{6,30},{7,31},{8,0},{9,1... | collective-permute-start | bytes 1966088 | tf_op jit(solution)/shard_map/ppermute | solution.py:35
  23.6 4.3 %collective-permute-done.6.refs_4_ = bf16[80,4096]{1,0:T(8,128)(2,1)S(1)} collective-permute-done((bf16[80,4096]{1,0:T(8,128)(2,1)S(1)}, bf16[80,4096]{1,0:T(8,128)(2,1)S(1)}, u32[]{:S(2)}, u32[]{:S(2)}) %collective-permute-start.6) | collective-permute-done | bytes 655392 | tf_op jit(solution)/shard_map/ppermute | solution.py:35
  27.9 6.5 %collective-permute-done.4 = bf16[80,4096]{1,0:T(8,128)(2,1)S(1)} collective-permute-done((bf16[80,4096]{1,0:T(8,128)(2,1)S(1)}, bf16[80,4096]{1,0:T(8,128)(2,1)S(1)}, u32[]{:S(2)}, u32[]{:S(2)}) %collective-permute-start.4) | collective-permute-done | bytes 655392 | tf_op jit(solution)/shard_map/ppermute | solution.py:86
  34.6 4.3 %collective-permute-done.7.refs_6_ = bf16[80,4096]{1,0:T(8,128)(2,1)S(1)} collective-permute-done((bf16[80,4096]{1,0:T(8,128)(2,1)S(1)}, bf16[80,4096]{1,0:T(8,128)(2,1)S(1)}, u32[]{:S(2)}, u32[]{:S(2)}) %collective-permute-start.7) | collective-permute-done | bytes 655392 | tf_op jit(solution)/shard_map/ppermute | solution.py:35
  40.3 3.6 %collective-permute-start.11 = (bf16[80,4096]{1,0:T(8,128)(2,1)S(1)}, bf16[80,4096]{1,0:T(8,128)(2,1)}, u32[]{:S(2)}, u32[]{:S(2)}) collective-permute-start(bf16[80,4096]{1,0:T(8,128)(2,1)S(1)} %order.1.refs_2_), channel_id=1, source_target_pairs={{0,2},{1,3},{2,0},{3,1},{4,6},{5,7},{6,4},{7,5},{8,10},{9,11},{10,... | collective-permute-start | bytes 1966088 | tf_op jit(solution)/shard_map/ppermute | solution.py:86
  43.9 6.4 %widen.2.refs_0_ = bf16[768,480]{1,0:T(8,128)(2,1)S(1)} custom-call(bf16[3,128,4096]{2,1,0:T(8,128)(2,1)S(1)} %pad_maximum_fusion.refs_0_.refs_1_, bf16[3,128,4096]{2,1,0:T(8,128)(2,1)} %collective-permute-done.refs_1_.refs_2_, bf16[80,4096]{1,0:T(8,128)(2,1)S(1)} %order.1.refs_2_, bf16[160,4096]{1,0:T(8,128)(2,1)S(1)} %pad_maximum_fusion.1.refs_3_, ...), custom_call_target="tpu_custom_call" | custom-call | flops 3019898880 | bytes 10485760 | tf_op jit(solution)/shard_map/widen/pallas_call | solution.py:217
  51.2 3.8 %collective-permute-done.11.refs_2_ = bf16[80,4096]{1,0:T(8,128)(2,1)} collective-permute-done((bf16[80,4096]{1,0:T(8,128)(2,1)S(1)}, bf16[80,4096]{1,0:T(8,128)(2,1)}, u32[]{:S(2)}, u32[]{:S(2)}) %collective-permute-start.11) | collective-permute-done | bytes 655392 | tf_op jit(solution)/shard_map/ppermute | solution.py:86
  55.7 2.0 %collective-permute-start.10 = (bf16[160,4096]{1,0:T(8,128)(2,1)}, bf16[160,4096]{1,0:T(8,128)(2,1)}, u32[]{:S(2)}, u32[]{:S(2)}) collective-permute-start(bf16[160,4096]{1,0:T(8,128)(2,1)} %collective-permute-done.9.refs_4_), channel_id=1, source_target_pairs={{0,24},{1,25},{2,26},{3,27},{4,28},{5,29},{6,30},{7,31},{8,0},{9,1... | collective-permute-start | bytes 3932168 | tf_op jit(solution)/shard_map/ppermute | solution.py:35
  58.0 6.0 %widen.3.refs_1_ = bf16[768,400]{1,0:T(8,128)(2,1)S(1)} custom-call(bf16[3,128,4096]{2,1,0:T(8,128)(2,1)S(1)} %pad_maximum_fusion.refs_0_.refs_1_, bf16[3,128,4096]{2,1,0:T(8,128)(2,1)} %collective-permute-done.refs_1_.refs_2_, bf16[80,4096]{1,0:T(8,128)(2,1)} %collective-permute-done.11.refs_2_, bf16[160,4096]{1,0:T(8,128)(2,1)S(1)} %collective-permute-done.14.refs_3_, ...), custom_call_target="tpu_custom_call" | custom-call | flops 2516582400 | bytes 10485760 | tf_op jit(solution)/shard_map/widen/pallas_call | solution.py:217
  64.8 1.5 collective-permute-done.12.refs_4_
  68.7 3.5 %spread.1.refs_7_ = bf16[64,128,128]{2,1,0:T(8,128)(2,1)S(1)} custom-call(s32[3]{0:T(128)S(1)} %pad_add_fusion.here.refs_0_, bf16[768,480]{1,0:T(8,128)(2,1)S(1)} %copy-done.8, bf16[768,400]{1,0:T(8,128)(2,1)S(1)} %copy-done.5), custom_call_target="tpu_custom_call" | custom-call | flops 1730150400 | bytes 4194304 | tf_op jit(solution)/shard_map/spread/pallas_call | solution.py:195
  72.2 7.6 %collective-permute-done.13.refs_5_ = bf16[80,4096]{1,0:T(8,128)(2,1)} collective-permute-done((bf16[80,4096]{1,0:T(8,128)(2,1)}, bf16[80,4096]{1,0:T(8,128)(2,1)}, u32[]{:S(2)}, u32[]{:S(2)}) %collective-permute-start.13) | collective-permute-done | bytes 655392 | tf_op jit(solution)/shard_map/ppermute | solution.py:35
  79.8 8.9 %widen_last.1 = bf16[64,128,128]{2,1,0:T(8,128)(2,1)S(1)} custom-call(s32[3]{0:T(128)S(1)} %pad_add_fusion.here.refs_0_, bf16[3,128,4096]{2,1,0:T(8,128)(2,1)S(1)} %pad_maximum_fusion.refs_0_.refs_1_, bf16[3,128,4096]{2,1,0:T(8,128)(2,1)} %collective-permute-done.refs_1_.refs_2_, bf16[160,4096]{1,0:T(8,128)(2,1)} %collective-permute-done.10.refs_3_, ...), custom_call_target="tpu_custom_call" | custom-call | flops 3303014400 | bytes 10485760 | tf_op jit(solution)/shard_map/widen_last/pallas_call | solution.py:217
  88.7 1.3 copy-done
  90.0 6.8 %all-to-all-start = ((bf16[32,2,128,128]{3,2,1,0:T(8,128)(2,1)}), bf16[32,2,128,128]{3,2,1,0:T(8,128)(2,1)}, u32[]{:S(2)}, u32[]{:S(2)}) async-start(bf16[32,2,128,128]{3,2,1,0:T(8,128)(2,1)} %bitcast.8), calls=%async_computation | async-start | bytes 4194304 | tf_op jit(solution)/shard_map/all_to_all | solution.py:401
  98.8 17.6 %all-to-all-done.z_ref = bf16[32,2,128,128]{3,2,1,0:T(8,128)(2,1)} async-done(((bf16[32,2,128,128]{3,2,1,0:T(8,128)(2,1)}), bf16[32,2,128,128]{3,2,1,0:T(8,128)(2,1)}, u32[]{:S(2)}, u32[]{:S(2)}) %all-to-all-start) | async-done | bytes 2097184 | tf_op jit(solution)/shard_map/all_to_all | solution.py:401
  116.4 1.3 copy-done.3
  117.7 5.3 %mix.1 = bf16[128,80,128]{2,1,0:T(8,128)(2,1)S(1)} custom-call(bf16[32,2,128,128]{3,2,1,0:T(8,128)(2,1)} %all-to-all-done.z_ref, bf16[2,640,512]{2,1,0:T(8,128)(2,1)S(1)} %copy-done.3), custom_call_target="tpu_custom_call" | custom-call | flops 2684354560 | bytes 8388608 | tf_op jit(solution)/shard_map/mix/pallas_call | solution.py:302
  123.1 1.5 copy-done.1
  124.6 17.7 %all-to-all-start.1 = ((bf16[128,80,128]{2,1,0:T(8,128)(2,1)}), bf16[128,80,128]{2,1,0:T(8,128)(2,1)S(1)}, u32[]{:S(2)}, u32[]{:S(2)}) async-start(bf16[128,80,128]{2,1,0:T(8,128)(2,1)} %copy-done.1), calls=%async_computation.1 | async-start | bytes 5242880 | tf_op jit(solution)/shard_map/all_to_all | solution.py:403
  142.5 35.5 %all-to-all-done.1 = bf16[128,80,128]{2,1,0:T(8,128)(2,1)S(1)} async-done(((bf16[128,80,128]{2,1,0:T(8,128)(2,1)}), bf16[128,80,128]{2,1,0:T(8,128)(2,1)S(1)}, u32[]{:S(2)}, u32[]{:S(2)}) %all-to-all-start.1) | async-done | bytes 2621472 | tf_op jit(solution)/shard_map/all_to_all | solution.py:403
  178.1 4.1 %depth.1 = (bf16[5,40,2560]{2,1,0:T(8,128)(2,1)}, f32[5,40,2560]{2,1,0:T(8,128)}, f32[5,40,2560]{2,1,0:T(8,128)}) custom-call(f32[5,4]{1,0:T(8,128)S(1)} %copy.15.depth, bf16[2,2,32,80,128]{4,3,2,1,0:T(8,128)(2,1)S(1)} %bitcast.7), custom_call_target="tpu_custom_call" | custom-call | flops 12582912 | bytes 8388608 | tf_op jit(solution)/shard_map/depth/pallas_call | solution.py:378
  (50 shorter events, 11.8 us)
Async XLA Ops:
  0.6 2.2 %copy-start.9 = (f32[1,128,4096]{2,1,0:T(8,128)S(1)}, f32[1,128,4096]{2,1,0:T(8,128)}, u32[]{:S(2)}) copy-start(f32[1,128,4096]{2,1,0:T(8,128)} %param.10) | copy-start | bytes 6291460
  2.9 1.2 copy-start.10
  4.1 1.8 %copy-start.6 = (bf16[20,4096]{1,0:T(8,128)(2,1)S(1)}, bf16[20,4096]{1,0:T(8,128)(2,1)}, u32[]{:S(2)}) copy-start(bf16[20,4096]{1,0:T(8,128)(2,1)} %own.1) | copy-start | bytes 491524
  4.4 34.4 %collective-permute-start = (bf16[3,128,4096]{2,1,0:T(8,128)(2,1)S(1)}, bf16[3,128,4096]{2,1,0:T(8,128)(2,1)}, u32[]{:S(2)}, u32[]{:S(2)}) collective-permute-start(bf16[3,128,4096]{2,1,0:T(8,128)(2,1)S(1)} %pad_maximum_fusion.refs_0_.refs_1_), channel_id=1, source_target_pairs={{0,32},{32,0},{1,33},{33,1},{2,34},{34,2},{3,35},{35,3},{4,36},{36... | collective-permute-start | bytes 9437192 | tf_op jit(solution)/shard_map/ppermute | solution.py:90
  5.9 6.0 %collective-permute-start.1 = (bf16[20,4096]{1,0:T(8,128)(2,1)S(1)}, bf16[20,4096]{1,0:T(8,128)(2,1)S(1)}, u32[]{:S(2)}, u32[]{:S(2)}) collective-permute-start(bf16[20,4096]{1,0:T(8,128)(2,1)S(1)} %copy-done.6), channel_id=1, source_target_pairs={{0,4},{1,5},{2,6},{3,7},{4,64},{5,65},{6,66},{7,67},{8,12},{9,13},... | collective-permute-start | bytes 491528 | tf_op jit(solution)/shard_map/ppermute | solution.py:35
  7.2 4.9 %collective-permute-start.2 = (bf16[20,4096]{1,0:T(8,128)(2,1)S(1)}, bf16[20,4096]{1,0:T(8,128)(2,1)}, u32[]{:S(2)}, u32[]{:S(2)}) collective-permute-start(bf16[20,4096]{1,0:T(8,128)(2,1)S(1)} %copy-done.6), channel_id=1, source_target_pairs={{0,68},{1,69},{2,70},{3,71},{4,0},{5,1},{6,2},{7,3},{8,76},{9,77},... | collective-permute-start | bytes 491528 | tf_op jit(solution)/shard_map/ppermute | solution.py:35
  8.6 6.6 %collective-permute-start.3 = (bf16[20,4096]{1,0:T(8,128)(2,1)S(1)}, bf16[20,4096]{1,0:T(8,128)(2,1)}, u32[]{:S(2)}, u32[]{:S(2)}) collective-permute-start(bf16[20,4096]{1,0:T(8,128)(2,1)S(1)} %copy-done.6), channel_id=1, source_target_pairs={{0,64},{1,65},{2,66},{3,67},{4,68},{5,69},{6,70},{7,71},{8,72},{9,... | collective-permute-start | bytes 491528 | tf_op jit(solution)/shard_map/ppermute | solution.py:35
  16.8 11.1 %collective-permute-start.6 = (bf16[80,4096]{1,0:T(8,128)(2,1)S(1)}, bf16[80,4096]{1,0:T(8,128)(2,1)S(1)}, u32[]{:S(2)}, u32[]{:S(2)}) collective-permute-start(bf16[80,4096]{1,0:T(8,128)(2,1)S(1)} %order.1.refs_2_), channel_id=1, source_target_pairs={{0,8},{1,9},{2,10},{3,11},{4,12},{5,13},{6,14},{7,15},{8,16},{9,17... | collective-permute-start | bytes 1966088 | tf_op jit(solution)/shard_map/ppermute | solution.py:35
  17.9 16.5 %collective-permute-start.4 = (bf16[80,4096]{1,0:T(8,128)(2,1)S(1)}, bf16[80,4096]{1,0:T(8,128)(2,1)S(1)}, u32[]{:S(2)}, u32[]{:S(2)}) collective-permute-start(bf16[80,4096]{1,0:T(8,128)(2,1)S(1)} %order.1.refs_2_), channel_id=1, source_target_pairs={{0,1},{1,2},{2,3},{3,0},{4,5},{5,6},{6,7},{7,4},{8,9},{9,10},{10,1... | collective-permute-start | bytes 1966088 | tf_op jit(solution)/shard_map/ppermute | solution.py:86
  19.6 14.9 %collective-permute-start.5 = (bf16[80,4096]{1,0:T(8,128)(2,1)S(1)}, bf16[80,4096]{1,0:T(8,128)(2,1)S(1)}, u32[]{:S(2)}, u32[]{:S(2)}) collective-permute-start(bf16[80,4096]{1,0:T(8,128)(2,1)S(1)} %order.1.refs_2_), channel_id=1, source_target_pairs={{0,3},{1,0},{2,1},{3,2},{4,7},{5,4},{6,5},{7,6},{8,11},{9,8},{10,9... | collective-permute-start | bytes 1966088 | tf_op jit(solution)/shard_map/ppermute | solution.py:86
  21.7 12.9 %collective-permute-start.8 = (bf16[80,4096]{1,0:T(8,128)(2,1)S(1)}, bf16[80,4096]{1,0:T(8,128)(2,1)S(1)}, u32[]{:S(2)}, u32[]{:S(2)}) collective-permute-start(bf16[80,4096]{1,0:T(8,128)(2,1)S(1)} %order.1.refs_2_), channel_id=1, source_target_pairs={{0,24},{1,25},{2,26},{3,27},{4,28},{5,29},{6,30},{7,31},{8,0},{9,1... | collective-permute-start | bytes 1966088 | tf_op jit(solution)/shard_map/ppermute | solution.py:35
  27.9 10.9 %collective-permute-start.7 = (bf16[80,4096]{1,0:T(8,128)(2,1)S(1)}, bf16[80,4096]{1,0:T(8,128)(2,1)S(1)}, u32[]{:S(2)}, u32[]{:S(2)}) collective-permute-start(bf16[80,4096]{1,0:T(8,128)(2,1)S(1)} %collective-permute-done.6.refs_4_), channel_id=1, source_target_pairs={{0,8},{1,9},{2,10},{3,11},{4,12},{5,13},{6,14},{7,15},{8,16},{9,17... | collective-permute-start | bytes 1966088 | tf_op jit(solution)/shard_map/ppermute | solution.py:35
  38.9 16.9 %collective-permute-start.9 = (bf16[160,4096]{1,0:T(8,128)(2,1)S(1)}, bf16[160,4096]{1,0:T(8,128)(2,1)}, u32[]{:S(2)}, u32[]{:S(2)}) collective-permute-start(bf16[160,4096]{1,0:T(8,128)(2,1)S(1)} %pad_maximum_fusion.1.refs_3_), channel_id=1, source_target_pairs={{0,24},{1,25},{2,26},{3,27},{4,28},{5,29},{6,30},{7,31},{8,0},{9,1... | collective-permute-start | bytes 3932168 | tf_op jit(solution)/shard_map/ppermute | solution.py:35
  39.1 18.8 %collective-permute-start.14 = (bf16[160,4096]{1,0:T(8,128)(2,1)S(1)}, bf16[160,4096]{1,0:T(8,128)(2,1)S(1)}, u32[]{:S(2)}, u32[]{:S(2)}) collective-permute-start(bf16[160,4096]{1,0:T(8,128)(2,1)S(1)} %pad_maximum_fusion.1.refs_3_), channel_id=1, source_target_pairs={{0,8},{1,9},{2,10},{3,11},{4,12},{5,13},{6,14},{7,15},{8,16},{9,17... | collective-permute-start | bytes 3932168 | tf_op jit(solution)/shard_map/ppermute | solution.py:35
  40.3 14.7 %collective-permute-start.11 = (bf16[80,4096]{1,0:T(8,128)(2,1)S(1)}, bf16[80,4096]{1,0:T(8,128)(2,1)}, u32[]{:S(2)}, u32[]{:S(2)}) collective-permute-start(bf16[80,4096]{1,0:T(8,128)(2,1)S(1)} %order.1.refs_2_), channel_id=1, source_target_pairs={{0,2},{1,3},{2,0},{3,1},{4,6},{5,7},{6,4},{7,5},{8,10},{9,11},{10,... | collective-permute-start | bytes 1966088 | tf_op jit(solution)/shard_map/ppermute | solution.py:86
  50.4 0.9 copy-start.7
  55.1 11.3 %collective-permute-start.12 = (bf16[80,4096]{1,0:T(8,128)(2,1)}, bf16[80,4096]{1,0:T(8,128)(2,1)}, u32[]{:S(2)}, u32[]{:S(2)}) collective-permute-start(bf16[80,4096]{1,0:T(8,128)(2,1)} %collective-permute-done.11.refs_2_), channel_id=1, source_target_pairs={{0,8},{1,9},{2,10},{3,11},{4,12},{5,13},{6,14},{7,15},{8,16},{9,17... | collective-permute-start | bytes 1966088 | tf_op jit(solution)/shard_map/ppermute | solution.py:35
  55.7 24.1 %collective-permute-start.10 = (bf16[160,4096]{1,0:T(8,128)(2,1)}, bf16[160,4096]{1,0:T(8,128)(2,1)}, u32[]{:S(2)}, u32[]{:S(2)}) collective-permute-start(bf16[160,4096]{1,0:T(8,128)(2,1)} %collective-permute-done.9.refs_4_), channel_id=1, source_target_pairs={{0,24},{1,25},{2,26},{3,27},{4,28},{5,29},{6,30},{7,31},{8,0},{9,1... | collective-permute-start | bytes 3932168 | tf_op jit(solution)/shard_map/ppermute | solution.py:35
  57.8 22.1 %collective-permute-start.13 = (bf16[80,4096]{1,0:T(8,128)(2,1)}, bf16[80,4096]{1,0:T(8,128)(2,1)}, u32[]{:S(2)}, u32[]{:S(2)}) collective-permute-start(bf16[80,4096]{1,0:T(8,128)(2,1)} %collective-permute-done.11.refs_2_), channel_id=1, source_target_pairs={{0,24},{1,25},{2,26},{3,27},{4,28},{5,29},{6,30},{7,31},{8,0},{9,1... | collective-permute-start | bytes 1966088 | tf_op jit(solution)/shard_map/ppermute | solution.py:35
  66.3 13.5 %collective-permute-start.15 = (bf16[80,4096]{1,0:T(8,128)(2,1)}, bf16[80,4096]{1,0:T(8,128)(2,1)}, u32[]{:S(2)}, u32[]{:S(2)}) collective-permute-start(bf16[80,4096]{1,0:T(8,128)(2,1)} %collective-permute-done.12.refs_4_), channel_id=1, source_target_pairs={{0,8},{1,9},{2,10},{3,11},{4,12},{5,13},{6,14},{7,15},{8,16},{9,17... | collective-permute-start | bytes 1966088 | tf_op jit(solution)/shard_map/ppermute | solution.py:35
  66.4 1.1 copy-start.5
  67.6 1.1 copy-start.8
  88.7 1.3 copy-start
  90.0 6.9 %copy-start.11 = (f32[40,32]{0,1:T(8,128)S(1)}, f32[40,32]{0,1:T(8,128)}, u32[]{:S(2)}) copy-start(f32[40,32]{0,1:T(8,128)} %param.12) | copy-start | bytes 15364
  90.0 26.4 %all-to-all-start = ((bf16[32,2,128,128]{3,2,1,0:T(8,128)(2,1)}), bf16[32,2,128,128]{3,2,1,0:T(8,128)(2,1)}, u32[]{:S(2)}, u32[]{:S(2)}) async-start(bf16[32,2,128,128]{3,2,1,0:T(8,128)(2,1)} %bitcast.8), calls=%async_computation | async-start | bytes 4194304 | tf_op jit(solution)/shard_map/all_to_all | solution.py:401
  97.7 1.1 copy-start.2
  116.4 1.3 copy-start.3
  123.1 1.5 copy-start.1
  124.6 17.8 %copy-start.12 = (f32[5,2]{0,1:T(2,128)S(1)}, f32[5,2]{0,1:T(2,128)}, u32[]{:S(2)}) copy-start(f32[5,2]{0,1:T(2,128)} %param.15) | copy-start | bytes 124
  124.6 17.8 %copy-start.13 = (s32[5,2]{0,1:T(2,128)S(1)}, s32[5,2]{0,1:T(2,128)}, u32[]{:S(2)}) copy-start(s32[5,2]{0,1:T(2,128)} %param.14) | copy-start | bytes 124
  124.6 17.8 %copy-start.14 = (s32[4]{0:T(128)S(1)}, s32[4]{0:T(128)}, u32[]{:S(2)}) copy-start(s32[4]{0:T(128)} %param.13) | copy-start | bytes 52
  124.6 53.5 %all-to-all-start.1 = ((bf16[128,80,128]{2,1,0:T(8,128)(2,1)}), bf16[128,80,128]{2,1,0:T(8,128)(2,1)S(1)}, u32[]{:S(2)}, u32[]{:S(2)}) async-start(bf16[128,80,128]{2,1,0:T(8,128)(2,1)} %copy-done.1), calls=%async_computation.1 | async-start | bytes 5242880 | tf_op jit(solution)/shard_map/all_to_all | solution.py:403
  (1 other events, 0.9 us)

commit v3 on v2

--- a/solution.py
+++ b/solution.py
@@ -92,7 +92,7 @@
     a_before, a_after = along_q(a, 1), along_q(a, -1)
     b_before, b_after = along_z(a, 1), along_z(a, -1)
     a_across = along_q(a_before, 1)
-    b = once(jnp.concatenate([b_before, b_after], axis=0), a_across, a_after, other)
+    b = once(jnp.concatenate([b_before, b_after], axis=0), a_before, a_after, other)
     d = along_z(once(a, b_before), 2)
     b_before, b_after = along_q(b, 1), along_q(b, -1)
     here = jnp.stack([core, q, z]).astype(jnp.int32)

time: 183 us -> 182 us (level)
  starting transfers between devices: 44.4 us -> 41.5 us
  waiting for transfers between devices: 86.9 us -> 89.5 us
    all_to_all x1, starting transfers between devices: 17.7 us -> 14.4 us  [on_device(): received = lax.all_to_all(y, AXES, split_axis=0, concat_axis=0, tiled=True)]
    ppermute x12, starting transfers between devices: 11 us -> 14.3 us  [shift(): return lax.ppermute(value, AXES, pairs)]
    all_to_all x1, waiting for transfers between devices: 17.6 us -> 20.2 us  [on_device(): z = lax.all_to_all(z, GROUP, split_axis=0, concat_axis=0, tiled=True)]
  transfers between devices with their start and end apart: 18 -> 18, of which waited for: 12 -> 10; matrix products, arithmetic and copies ran while one was open for 0% -> 0% of each run, Pallas kernels for 10% -> 10%
where the time goes in v3:
time: 182 us
  waiting for transfers between devices  89.5 us (49%)
  starting transfers between devices  41.5 us (23%)
  Pallas kernels  36.6 us (20%)
  local copies, waits for them, and re-layouts  10.8 us (6%)
  other arithmetic  2.59 us (1%)
    all_to_all x1, waiting for transfers between devices, on_device(): received = lax.all_to_all(y, AXES, split_axis=0, concat_axis=0, tiled=True)  35.5 us
    ppermute x12, waiting for transfers between devices, shift(): return lax.ppermute(value, AXES, pairs)  23.4 us
    pallas_call x3, Pallas kernels, project_call(): pl.pallas_call(kernel, out_shape=jax.ShapeDtypeStruct(out, BF16), in_spec...  21.3 us
    all_to_all x1, waiting for transfers between devices, on_device(): z = lax.all_to_all(z, GROUP, split_axis=0, concat_axis=0, tiled=True)  20.2 us
    all_to_all x1, starting transfers between devices, on_device(): received = lax.all_to_all(y, AXES, split_axis=0, concat_axis=0, tiled=True)  14.4 us
    ppermute x12, starting transfers between devices, shift(): return lax.ppermute(value, AXES, pairs)  14.3 us
    unnamed x31, local copies, waits for them, and re-layouts  10.7 us
    ppermute x3, waiting for transfers between devices, along_z(): return lax.ppermute(value, 'z', [(i, (i + by) % 4) for i in range(4)])  10.4 us
  transfers between devices with their start and end apart: 18, of which 10 were waited for; matrix products, arithmetic and copies ran while one was open for 0% of the time, Pallas kernels for 10%

profile of v3, /device:TPU:1, one launch (start us, length us, event | category | flops | bytes accessed | tf_op | source)
XLA Modules:
  0.0 181.8 jit_solution(15436407791171939679)
XLA Ops:
  0.6 1.9 %convert_element_type.8 = bf16[1,128,4096]{2,1,0:T(8,128)(2,1)S(1)} convert(f32[1,128,4096]{2,1,0:T(8,128)} %param.9) | non-fusion elementwise | flops 524288 | bytes 3145728 | tf_op jit(solution)/shard_map/convert_element_type | solution.py:89
  4.4 1.5 collective-permute-start
  5.9 1.3 collective-permute-start.1
  7.2 1.4 collective-permute-start.2
  8.6 1.6 collective-permute-start.3
  10.2 1.7 collective-permute-done.1.before
  12.1 3.1 %collective-permute-done.3.across = bf16[20,4096]{1,0:T(8,128)(2,1)} collective-permute-done((bf16[20,4096]{1,0:T(8,128)(2,1)S(1)}, bf16[20,4096]{1,0:T(8,128)(2,1)}, u32[]{:S(2)}, u32[]{:S(2)}) %collective-permute-start.3) | collective-permute-done | bytes 163872 | tf_op jit(solution)/shard_map/ppermute | solution.py:35
  15.2 1.6 order.1.refs_2_
  16.8 1.7 collective-permute-start.4
  18.6 2.2 %collective-permute-start.5 = (bf16[80,4096]{1,0:T(8,128)(2,1)S(1)}, bf16[80,4096]{1,0:T(8,128)(2,1)S(1)}, u32[]{:S(2)}, u32[]{:S(2)}) collective-permute-start(bf16[80,4096]{1,0:T(8,128)(2,1)S(1)} %order.1.refs_2_), channel_id=1, source_target_pairs={{0,3},{1,0},{2,1},{3,2},{4,7},{5,4},{6,5},{7,6},{8,11},{9,8},{10,9... | collective-permute-start | bytes 1966088 | tf_op jit(solution)/shard_map/ppermute | solution.py:86
  21.8 1.7 collective-permute-start.7
  23.5 10.4 %collective-permute-done.4 = bf16[80,4096]{1,0:T(8,128)(2,1)S(1)} collective-permute-done((bf16[80,4096]{1,0:T(8,128)(2,1)S(1)}, bf16[80,4096]{1,0:T(8,128)(2,1)S(1)}, u32[]{:S(2)}, u32[]{:S(2)}) %collective-permute-start.4) | collective-permute-done | bytes 655392 | tf_op jit(solution)/shard_map/ppermute | solution.py:86
  34.1 4.1 %collective-permute-start.8 = (bf16[160,4096]{1,0:T(8,128)(2,1)S(1)}, bf16[160,4096]{1,0:T(8,128)(2,1)}, u32[]{:S(2)}, u32[]{:S(2)}) collective-permute-start(bf16[160,4096]{1,0:T(8,128)(2,1)S(1)} %pad_maximum_fusion.1.refs_3_), channel_id=1, source_target_pairs={{0,24},{1,25},{2,26},{3,27},{4,28},{5,29},{6,30},{7,31},{8,0},{9,1... | collective-permute-start | bytes 3932168 | tf_op jit(solution)/shard_map/ppermute | solution.py:35
  38.2 2.0 %collective-permute-start.10 = (bf16[80,4096]{1,0:T(8,128)(2,1)S(1)}, bf16[80,4096]{1,0:T(8,128)(2,1)}, u32[]{:S(2)}, u32[]{:S(2)}) collective-permute-start(bf16[80,4096]{1,0:T(8,128)(2,1)S(1)} %order.1.refs_2_), channel_id=1, source_target_pairs={{0,2},{1,3},{2,0},{3,1},{4,6},{5,7},{6,4},{7,5},{8,10},{9,11},{10,... | collective-permute-start | bytes 1966088 | tf_op jit(solution)/shard_map/ppermute | solution.py:86
  40.2 9.0 %collective-permute-done.11.refs_6_ = bf16[80,4096]{1,0:T(8,128)(2,1)S(1)} collective-permute-done((bf16[80,4096]{1,0:T(8,128)(2,1)S(1)}, bf16[80,4096]{1,0:T(8,128)(2,1)S(1)}, u32[]{:S(2)}, u32[]{:S(2)}) %collective-permute-start.11) | collective-permute-done | bytes 655392 | tf_op jit(solution)/shard_map/ppermute | solution.py:35
  49.3 6.4 %widen.2.refs_0_ = bf16[768,480]{1,0:T(8,128)(2,1)S(1)} custom-call(bf16[3,128,4096]{2,1,0:T(8,128)(2,1)S(1)} %pad_maximum_fusion.refs_0_.refs_1_, bf16[3,128,4096]{2,1,0:T(8,128)(2,1)} %collective-permute-done.refs_1_.refs_2_, bf16[80,4096]{1,0:T(8,128)(2,1)S(1)} %order.1.refs_2_, bf16[160,4096]{1,0:T(8,128)(2,1)S(1)} %pad_maximum_fusion.1.refs_3_, ...), custom_call_target="tpu_custom_call" | custom-call | flops 3019898880 | bytes 10485760 | tf_op jit(solution)/shard_map/widen/pallas_call | solution.py:217
  56.6 2.7 %collective-permute-start.9 = (bf16[160,4096]{1,0:T(8,128)(2,1)}, bf16[160,4096]{1,0:T(8,128)(2,1)}, u32[]{:S(2)}, u32[]{:S(2)}) collective-permute-start(bf16[160,4096]{1,0:T(8,128)(2,1)} %collective-permute-done.8.refs_4_), channel_id=1, source_target_pairs={{0,24},{1,25},{2,26},{3,27},{4,28},{5,29},{6,30},{7,31},{8,0},{9,1... | collective-permute-start | bytes 3932168 | tf_op jit(solution)/shard_map/ppermute | solution.py:35
  59.7 3.5 %collective-permute-done.14.refs_3_ = bf16[160,4096]{1,0:T(8,128)(2,1)S(1)} collective-permute-done((bf16[160,4096]{1,0:T(8,128)(2,1)S(1)}, bf16[160,4096]{1,0:T(8,128)(2,1)S(1)}, u32[]{:S(2)}, u32[]{:S(2)}) %collective-permute-start.14) | collective-permute-done | bytes 1310752 | tf_op jit(solution)/shard_map/ppermute | solution.py:35
  63.2 6.0 %widen.3.refs_1_ = bf16[768,400]{1,0:T(8,128)(2,1)S(1)} custom-call(bf16[3,128,4096]{2,1,0:T(8,128)(2,1)S(1)} %pad_maximum_fusion.refs_0_.refs_1_, bf16[3,128,4096]{2,1,0:T(8,128)(2,1)} %collective-permute-done.refs_1_.refs_2_, bf16[80,4096]{1,0:T(8,128)(2,1)} %collective-permute-done.10.refs_2_, bf16[160,4096]{1,0:T(8,128)(2,1)S(1)} %collective-permute-done.14.refs_3_, ...), custom_call_target="tpu_custom_call" | custom-call | flops 2516582400 | bytes 10485760 | tf_op jit(solution)/shard_map/widen/pallas_call | solution.py:217
  70.4 1.1 copy-done.5
  72.7 3.5 %spread.1.refs_7_ = bf16[64,128,128]{2,1,0:T(8,128)(2,1)S(1)} custom-call(s32[3]{0:T(128)S(1)} %pad_add_fusion.here.refs_0_, bf16[768,480]{1,0:T(8,128)(2,1)S(1)} %copy-done.8, bf16[768,400]{1,0:T(8,128)(2,1)S(1)} %copy-done.5), custom_call_target="tpu_custom_call" | custom-call | flops 1730150400 | bytes 4194304 | tf_op jit(solution)/shard_map/spread/pallas_call | solution.py:195
  76.2 5.5 %collective-permute-done.13.refs_5_ = bf16[80,4096]{1,0:T(8,128)(2,1)} collective-permute-done((bf16[80,4096]{1,0:T(8,128)(2,1)}, bf16[80,4096]{1,0:T(8,128)(2,1)}, u32[]{:S(2)}, u32[]{:S(2)}) %collective-permute-start.13) | collective-permute-done | bytes 655392 | tf_op jit(solution)/shard_map/ppermute | solution.py:35
  81.7 8.9 %widen_last.1 = bf16[64,128,128]{2,1,0:T(8,128)(2,1)S(1)} custom-call(s32[3]{0:T(128)S(1)} %pad_add_fusion.here.refs_0_, bf16[3,128,4096]{2,1,0:T(8,128)(2,1)S(1)} %pad_maximum_fusion.refs_0_.refs_1_, bf16[3,128,4096]{2,1,0:T(8,128)(2,1)} %collective-permute-done.refs_1_.refs_2_, bf16[160,4096]{1,0:T(8,128)(2,1)} %collective-permute-done.9.refs_3_, ...), custom_call_target="tpu_custom_call" | custom-call | flops 3303014400 | bytes 10485760 | tf_op jit(solution)/shard_map/widen_last/pallas_call | solution.py:217
  90.6 1.3 copy-done
  91.9 5.4 %all-to-all-start = ((bf16[32,2,128,128]{3,2,1,0:T(8,128)(2,1)}), bf16[32,2,128,128]{3,2,1,0:T(8,128)(2,1)}, u32[]{:S(2)}, u32[]{:S(2)}) async-start(bf16[32,2,128,128]{3,2,1,0:T(8,128)(2,1)} %bitcast.8), calls=%async_computation | async-start | bytes 4194304 | tf_op jit(solution)/shard_map/all_to_all | solution.py:401
  99.3 20.2 %all-to-all-done.z_ref = bf16[32,2,128,128]{3,2,1,0:T(8,128)(2,1)} async-done(((bf16[32,2,128,128]{3,2,1,0:T(8,128)(2,1)}), bf16[32,2,128,128]{3,2,1,0:T(8,128)(2,1)}, u32[]{:S(2)}, u32[]{:S(2)}) %all-to-all-start) | async-done | bytes 2097184 | tf_op jit(solution)/shard_map/all_to_all | solution.py:401
  119.5 1.3 copy-done.3
  120.8 5.3 %mix.1 = bf16[128,80,128]{2,1,0:T(8,128)(2,1)S(1)} custom-call(bf16[32,2,128,128]{3,2,1,0:T(8,128)(2,1)} %all-to-all-done.z_ref, bf16[2,640,512]{2,1,0:T(8,128)(2,1)S(1)} %copy-done.3), custom_call_target="tpu_custom_call" | custom-call | flops 2684354560 | bytes 8388608 | tf_op jit(solution)/shard_map/mix/pallas_call | solution.py:302
  126.1 1.5 copy-done.1
  127.6 14.4 %all-to-all-start.1 = ((bf16[128,80,128]{2,1,0:T(8,128)(2,1)}), bf16[128,80,128]{2,1,0:T(8,128)(2,1)S(1)}, u32[]{:S(2)}, u32[]{:S(2)}) async-start(bf16[128,80,128]{2,1,0:T(8,128)(2,1)} %copy-done.1), calls=%async_computation.1 | async-start | bytes 5242880 | tf_op jit(solution)/shard_map/all_to_all | solution.py:403
  142.2 35.5 %all-to-all-done.1 = bf16[128,80,128]{2,1,0:T(8,128)(2,1)S(1)} async-done(((bf16[128,80,128]{2,1,0:T(8,128)(2,1)}), bf16[128,80,128]{2,1,0:T(8,128)(2,1)S(1)}, u32[]{:S(2)}, u32[]{:S(2)}) %all-to-all-start.1) | async-done | bytes 2621472 | tf_op jit(solution)/shard_map/all_to_all | solution.py:403
  177.7 4.1 %depth.1 = (bf16[5,40,2560]{2,1,0:T(8,128)(2,1)}, f32[5,40,2560]{2,1,0:T(8,128)}, f32[5,40,2560]{2,1,0:T(8,128)}) custom-call(f32[5,4]{1,0:T(8,128)S(1)} %copy.15.depth, bf16[2,2,32,80,128]{4,3,2,1,0:T(8,128)(2,1)S(1)} %bitcast.7), custom_call_target="tpu_custom_call" | custom-call | flops 12582912 | bytes 8388608 | tf_op jit(solution)/shard_map/depth/pallas_call | solution.py:378
  (50 shorter events, 9.0 us)
Async XLA Ops:
  0.6 2.2 %copy-start.9 = (f32[1,128,4096]{2,1,0:T(8,128)S(1)}, f32[1,128,4096]{2,1,0:T(8,128)}, u32[]{:S(2)}) copy-start(f32[1,128,4096]{2,1,0:T(8,128)} %param.10) | copy-start | bytes 6291460
  2.9 1.2 copy-start.10
  4.1 1.8 %copy-start.6 = (bf16[20,4096]{1,0:T(8,128)(2,1)S(1)}, bf16[20,4096]{1,0:T(8,128)(2,1)}, u32[]{:S(2)}) copy-start(bf16[20,4096]{1,0:T(8,128)(2,1)} %own.1) | copy-start | bytes 491524
  4.4 29.7 %collective-permute-start = (bf16[3,128,4096]{2,1,0:T(8,128)(2,1)S(1)}, bf16[3,128,4096]{2,1,0:T(8,128)(2,1)}, u32[]{:S(2)}, u32[]{:S(2)}) collective-permute-start(bf16[3,128,4096]{2,1,0:T(8,128)(2,1)S(1)} %pad_maximum_fusion.refs_0_.refs_1_), channel_id=1, source_target_pairs={{0,32},{32,0},{1,33},{33,1},{2,34},{34,2},{3,35},{35,3},{4,36},{36... | collective-permute-start | bytes 9437192 | tf_op jit(solution)/shard_map/ppermute | solution.py:90
  5.9 6.0 %collective-permute-start.1 = (bf16[20,4096]{1,0:T(8,128)(2,1)S(1)}, bf16[20,4096]{1,0:T(8,128)(2,1)S(1)}, u32[]{:S(2)}, u32[]{:S(2)}) collective-permute-start(bf16[20,4096]{1,0:T(8,128)(2,1)S(1)} %copy-done.6), channel_id=1, source_target_pairs={{0,4},{1,5},{2,6},{3,7},{4,64},{5,65},{6,66},{7,67},{8,12},{9,13},... | collective-permute-start | bytes 491528 | tf_op jit(solution)/shard_map/ppermute | solution.py:35
  7.2 4.9 %collective-permute-start.2 = (bf16[20,4096]{1,0:T(8,128)(2,1)S(1)}, bf16[20,4096]{1,0:T(8,128)(2,1)}, u32[]{:S(2)}, u32[]{:S(2)}) collective-permute-start(bf16[20,4096]{1,0:T(8,128)(2,1)S(1)} %copy-done.6), channel_id=1, source_target_pairs={{0,68},{1,69},{2,70},{3,71},{4,0},{5,1},{6,2},{7,3},{8,76},{9,77},... | collective-permute-start | bytes 491528 | tf_op jit(solution)/shard_map/ppermute | solution.py:35
  8.6 6.6 %collective-permute-start.3 = (bf16[20,4096]{1,0:T(8,128)(2,1)S(1)}, bf16[20,4096]{1,0:T(8,128)(2,1)}, u32[]{:S(2)}, u32[]{:S(2)}) collective-permute-start(bf16[20,4096]{1,0:T(8,128)(2,1)S(1)} %copy-done.6), channel_id=1, source_target_pairs={{0,64},{1,65},{2,66},{3,67},{4,68},{5,69},{6,70},{7,71},{8,72},{9,... | collective-permute-start | bytes 491528 | tf_op jit(solution)/shard_map/ppermute | solution.py:35
  16.8 17.1 %collective-permute-start.4 = (bf16[80,4096]{1,0:T(8,128)(2,1)S(1)}, bf16[80,4096]{1,0:T(8,128)(2,1)S(1)}, u32[]{:S(2)}, u32[]{:S(2)}) collective-permute-start(bf16[80,4096]{1,0:T(8,128)(2,1)S(1)} %order.1.refs_2_), channel_id=1, source_target_pairs={{0,1},{1,2},{2,3},{3,0},{4,5},{5,6},{6,7},{7,4},{8,9},{9,10},{10,1... | collective-permute-start | bytes 1966088 | tf_op jit(solution)/shard_map/ppermute | solution.py:86
  18.6 15.4 %collective-permute-start.5 = (bf16[80,4096]{1,0:T(8,128)(2,1)S(1)}, bf16[80,4096]{1,0:T(8,128)(2,1)S(1)}, u32[]{:S(2)}, u32[]{:S(2)}) collective-permute-start(bf16[80,4096]{1,0:T(8,128)(2,1)S(1)} %order.1.refs_2_), channel_id=1, source_target_pairs={{0,3},{1,0},{2,1},{3,2},{4,7},{5,4},{6,5},{7,6},{8,11},{9,8},{10,9... | collective-permute-start | bytes 1966088 | tf_op jit(solution)/shard_map/ppermute | solution.py:86
  20.8 13.3 %collective-permute-start.6 = (bf16[80,4096]{1,0:T(8,128)(2,1)S(1)}, bf16[80,4096]{1,0:T(8,128)(2,1)S(1)}, u32[]{:S(2)}, u32[]{:S(2)}) collective-permute-start(bf16[80,4096]{1,0:T(8,128)(2,1)S(1)} %order.1.refs_2_), channel_id=1, source_target_pairs={{0,8},{1,9},{2,10},{3,11},{4,12},{5,13},{6,14},{7,15},{8,16},{9,17... | collective-permute-start | bytes 1966088 | tf_op jit(solution)/shard_map/ppermute | solution.py:35
  21.8 12.3 %collective-permute-start.7 = (bf16[80,4096]{1,0:T(8,128)(2,1)S(1)}, bf16[80,4096]{1,0:T(8,128)(2,1)S(1)}, u32[]{:S(2)}, u32[]{:S(2)}) collective-permute-start(bf16[80,4096]{1,0:T(8,128)(2,1)S(1)} %order.1.refs_2_), channel_id=1, source_target_pairs={{0,24},{1,25},{2,26},{3,27},{4,28},{5,29},{6,30},{7,31},{8,0},{9,1... | collective-permute-start | bytes 1966088 | tf_op jit(solution)/shard_map/ppermute | solution.py:35
  34.1 22.5 %collective-permute-start.8 = (bf16[160,4096]{1,0:T(8,128)(2,1)S(1)}, bf16[160,4096]{1,0:T(8,128)(2,1)}, u32[]{:S(2)}, u32[]{:S(2)}) collective-permute-start(bf16[160,4096]{1,0:T(8,128)(2,1)S(1)} %pad_maximum_fusion.1.refs_3_), channel_id=1, source_target_pairs={{0,24},{1,25},{2,26},{3,27},{4,28},{5,29},{6,30},{7,31},{8,0},{9,1... | collective-permute-start | bytes 3932168 | tf_op jit(solution)/shard_map/ppermute | solution.py:35
  38.2 11.0 %collective-permute-start.11 = (bf16[80,4096]{1,0:T(8,128)(2,1)S(1)}, bf16[80,4096]{1,0:T(8,128)(2,1)S(1)}, u32[]{:S(2)}, u32[]{:S(2)}) collective-permute-start(bf16[80,4096]{1,0:T(8,128)(2,1)S(1)} %collective-permute-done.6.refs_4_), channel_id=1, source_target_pairs={{0,8},{1,9},{2,10},{3,11},{4,12},{5,13},{6,14},{7,15},{8,16},{9,17... | collective-permute-start | bytes 1966088 | tf_op jit(solution)/shard_map/ppermute | solution.py:35
  38.2 25.0 %collective-permute-start.14 = (bf16[160,4096]{1,0:T(8,128)(2,1)S(1)}, bf16[160,4096]{1,0:T(8,128)(2,1)S(1)}, u32[]{:S(2)}, u32[]{:S(2)}) collective-permute-start(bf16[160,4096]{1,0:T(8,128)(2,1)S(1)} %pad_maximum_fusion.1.refs_3_), channel_id=1, source_target_pairs={{0,8},{1,9},{2,10},{3,11},{4,12},{5,13},{6,14},{7,15},{8,16},{9,17... | collective-permute-start | bytes 3932168 | tf_op jit(solution)/shard_map/ppermute | solution.py:35
  38.2 18.3 %collective-permute-start.10 = (bf16[80,4096]{1,0:T(8,128)(2,1)S(1)}, bf16[80,4096]{1,0:T(8,128)(2,1)}, u32[]{:S(2)}, u32[]{:S(2)}) collective-permute-start(bf16[80,4096]{1,0:T(8,128)(2,1)S(1)} %order.1.refs_2_), channel_id=1, source_target_pairs={{0,2},{1,3},{2,0},{3,1},{4,6},{5,7},{6,4},{7,5},{8,10},{9,11},{10,... | collective-permute-start | bytes 1966088 | tf_op jit(solution)/shard_map/ppermute | solution.py:86
  55.7 0.9 copy-start.7
  56.6 13.8 %collective-permute-start.12 = (bf16[80,4096]{1,0:T(8,128)(2,1)}, bf16[80,4096]{1,0:T(8,128)(2,1)}, u32[]{:S(2)}, u32[]{:S(2)}) collective-permute-start(bf16[80,4096]{1,0:T(8,128)(2,1)} %collective-permute-done.10.refs_2_), channel_id=1, source_target_pairs={{0,8},{1,9},{2,10},{3,11},{4,12},{5,13},{6,14},{7,15},{8,16},{9,17... | collective-permute-start | bytes 1966088 | tf_op jit(solution)/shard_map/ppermute | solution.py:35
  56.6 25.1 %collective-permute-start.9 = (bf16[160,4096]{1,0:T(8,128)(2,1)}, bf16[160,4096]{1,0:T(8,128)(2,1)}, u32[]{:S(2)}, u32[]{:S(2)}) collective-permute-start(bf16[160,4096]{1,0:T(8,128)(2,1)} %collective-permute-done.8.refs_4_), channel_id=1, source_target_pairs={{0,24},{1,25},{2,26},{3,27},{4,28},{5,29},{6,30},{7,31},{8,0},{9,1... | collective-permute-start | bytes 3932168 | tf_op jit(solution)/shard_map/ppermute | solution.py:35
  59.2 22.5 %collective-permute-start.13 = (bf16[80,4096]{1,0:T(8,128)(2,1)}, bf16[80,4096]{1,0:T(8,128)(2,1)}, u32[]{:S(2)}, u32[]{:S(2)}) collective-permute-start(bf16[80,4096]{1,0:T(8,128)(2,1)} %collective-permute-done.10.refs_2_), channel_id=1, source_target_pairs={{0,24},{1,25},{2,26},{3,27},{4,28},{5,29},{6,30},{7,31},{8,0},{9,1... | collective-permute-start | bytes 1966088 | tf_op jit(solution)/shard_map/ppermute | solution.py:35
  70.3 11.4 %collective-permute-start.15 = (bf16[80,4096]{1,0:T(8,128)(2,1)}, bf16[80,4096]{1,0:T(8,128)(2,1)}, u32[]{:S(2)}, u32[]{:S(2)}) collective-permute-start(bf16[80,4096]{1,0:T(8,128)(2,1)} %collective-permute-done.12.refs_4_), channel_id=1, source_target_pairs={{0,8},{1,9},{2,10},{3,11},{4,12},{5,13},{6,14},{7,15},{8,16},{9,17... | collective-permute-start | bytes 1966088 | tf_op jit(solution)/shard_map/ppermute | solution.py:35
  70.4 1.1 copy-start.5
  71.5 1.1 copy-start.8
  90.6 1.3 copy-start
  91.9 5.5 %copy-start.11 = (f32[40,32]{0,1:T(8,128)S(1)}, f32[40,32]{0,1:T(8,128)}, u32[]{:S(2)}) copy-start(f32[40,32]{0,1:T(8,128)} %param.12) | copy-start | bytes 15364
  91.9 27.5 %all-to-all-start = ((bf16[32,2,128,128]{3,2,1,0:T(8,128)(2,1)}), bf16[32,2,128,128]{3,2,1,0:T(8,128)(2,1)}, u32[]{:S(2)}, u32[]{:S(2)}) async-start(bf16[32,2,128,128]{3,2,1,0:T(8,128)(2,1)} %bitcast.8), calls=%async_computation | async-start | bytes 4194304 | tf_op jit(solution)/shard_map/all_to_all | solution.py:401
  98.2 1.1 copy-start.2
  119.5 1.3 copy-start.3
  126.1 1.5 copy-start.1
  127.6 14.4 %copy-start.12 = (f32[5,2]{0,1:T(2,128)S(1)}, f32[5,2]{0,1:T(2,128)}, u32[]{:S(2)}) copy-start(f32[5,2]{0,1:T(2,128)} %param.15) | copy-start | bytes 124
  127.6 14.4 %copy-start.13 = (s32[5,2]{0,1:T(2,128)S(1)}, s32[5,2]{0,1:T(2,128)}, u32[]{:S(2)}) copy-start(s32[5,2]{0,1:T(2,128)} %param.14) | copy-start | bytes 124
  127.6 14.4 %copy-start.14 = (s32[4]{0:T(128)S(1)}, s32[4]{0:T(128)}, u32[]{:S(2)}) copy-start(s32[4]{0:T(128)} %param.13) | copy-start | bytes 52
  127.6 50.1 %all-to-all-start.1 = ((bf16[128,80,128]{2,1,0:T(8,128)(2,1)}), bf16[128,80,128]{2,1,0:T(8,128)(2,1)S(1)}, u32[]{:S(2)}, u32[]{:S(2)}) async-start(bf16[128,80,128]{2,1,0:T(8,128)(2,1)} %copy-done.1), calls=%async_computation.1 | async-start | bytes 5242880 | tf_op jit(solution)/shard_map/all_to_all | solution.py:403
  (1 other events, 0.9 us)

commit v4 on v3

--- a/solution.py
+++ b/solution.py
@@ -282,7 +282,6 @@
             [z_ref[:, k, pl.ds(row + 16 * i, 16), :].reshape(512, 128) for i in range(2)], axis=1
         )
         y = jnp.dot(m_ref[0], block, preferred_element_type=F32)
-        y = y + jnp.dot(m_ref[1], block, preferred_element_type=F32)
         for g in range(40):
             for i in range(2):
                 y_ref[k, pl.ds(g * 128 + row + 16 * i, 16), :] = y[
@@ -311,7 +310,7 @@
         scratch_shapes=[pltpu.VMEM((2, 5120, 128), F32)],
         compiler_params=pltpu.CompilerParams(vmem_limit_bytes=VMEM),
         cost_estimate=pl.CostEstimate(
-            flops=16 * 4 * 640 * 512 * 128, bytes_accessed=8 << 20, transcendentals=0
+            flops=16 * 2 * 640 * 512 * 128, bytes_accessed=8 << 20, transcendentals=0
         ),
         name="mix",
     )(z, matrices)
@@ -320,8 +319,6 @@
 def matrix_kernel(squared, head, out):
     h = head[...]
     h = jnp.where(squared[0] == 1, h * h, h)
-    high = h.astype(BF16)
-    low = (h - high.astype(F32)).astype(BF16)
 
     def iota(shape, dim):
         return lax.broadcasted_iota(jnp.int32, shape, dim)
@@ -329,10 +326,9 @@
     down = (iota((640, 40), 0) // 16 == iota((640, 40), 1)).astype(BF16)
     along = (iota((32, 512), 1) // 16 == iota((32, 512), 0)).astype(BF16)
     same = iota((640, 512), 0) % 16 == iota((640, 512), 1) % 16
-    for i, part in enumerate((high, low)):
-        tall = jnp.dot(down, part, preferred_element_type=F32).astype(BF16)
-        full = jnp.dot(tall, along, preferred_element_type=F32)
-        out[i] = jnp.where(same, full, 0.0).astype(BF16)
+    tall = jnp.dot(down, h.astype(BF16), preferred_element_type=F32).astype(BF16)
+    full = jnp.dot(tall, along, preferred_element_type=F32)
+    out[0] = jnp.where(same, full, 0.0).astype(BF16)
 
 
 def mixing_matrices(head_map):
@@ -341,7 +337,7 @@
     whole = pl.BlockSpec(memory_space=pltpu.VMEM)
     return pl.pallas_call(
         matrix_kernel,
-        out_shape=jax.ShapeDtypeStruct((2, 640, 512), BF16),
+        out_shape=jax.ShapeDtypeStruct((1, 640, 512), BF16),
         in_specs=[pl.BlockSpec(memory_space=pltpu.SMEM), whole],
         out_specs=whole,
         compiler_params=pltpu.CompilerParams(vmem_limit_bytes=VMEM),

time: 182 us -> 182 us (level)
  Pallas kernels: 36.6 us -> 33.3 us
  local copies, waits for them, and re-layouts: 10.8 us -> 13.3 us
    pallas_call x1, Pallas kernels: 5.33 us -> 2.37 us  [mix(): pl.pallas_call(mix_kernel, out_shape=jax.ShapeDtypeStruct((128, 80, 128),...]
    unnamed x31 -> x35, local copies, waits for them, and re-layouts: 10.7 us -> 13.2 us
where the time goes in v4:
time: 182 us; the launch traced here: 181 us
  waiting for transfers between devices  90 us (49%)
  starting transfers between devices  41.3 us (23%)
  Pallas kernels  33.3 us (18%)
  local copies, waits for them, and re-layouts  13.3 us (7%)
  other arithmetic  2.59 us (1%)
    all_to_all x1, waiting for transfers between devices, on_device(): received = lax.all_to_all(y, AXES, split_axis=0, concat_axis=0, tiled=True)  35.5 us
    ppermute x12, waiting for transfers between devices, shift(): return lax.ppermute(value, AXES, pairs)  23.4 us
    pallas_call x3, Pallas kernels, project_call(): pl.pallas_call(kernel, out_shape=jax.ShapeDtypeStruct(out, BF16), in_spec...  21.3 us
    all_to_all x1, waiting for transfers between devices, on_device(): z = lax.all_to_all(z, GROUP, split_axis=0, concat_axis=0, tiled=True)  20.7 us
    all_to_all x1, starting transfers between devices, on_device(): received = lax.all_to_all(y, AXES, split_axis=0, concat_axis=0, tiled=True)  14.4 us
    ppermute x12, starting transfers between devices, shift(): return lax.ppermute(value, AXES, pairs)  14.3 us
    unnamed x35, local copies, waits for them, and re-layouts  13.2 us
    ppermute x3, waiting for transfers between devices, along_z(): return lax.ppermute(value, 'z', [(i, (i + by) % 4) for i in range(4)])  10.4 us
  transfers between devices with their start and end apart: 18, of which 10 were waited for; matrix products, arithmetic and copies ran while one was open for 0% of the time, Pallas kernels for 10%

profile of v4, /device:TPU:1, one launch (start us, length us, event | category | flops | bytes accessed | tf_op | source)
XLA Modules:
  0.0 181.5 jit_solution(7553724648893350397)
XLA Ops:
  0.6 1.9 %convert_element_type.8 = bf16[1,128,4096]{2,1,0:T(8,128)(2,1)S(1)} convert(f32[1,128,4096]{2,1,0:T(8,128)} %param.9) | non-fusion elementwise | flops 524288 | bytes 3145728 | tf_op jit(solution)/shard_map/convert_element_type | solution.py:89
  4.4 1.5 collective-permute-start
  5.9 1.3 collective-permute-start.1
  7.2 1.4 collective-permute-start.2
  8.6 1.6 collective-permute-start.3
  10.2 1.7 collective-permute-done.1.before
  12.1 3.1 %collective-permute-done.3.across = bf16[20,4096]{1,0:T(8,128)(2,1)} collective-permute-done((bf16[20,4096]{1,0:T(8,128)(2,1)S(1)}, bf16[20,4096]{1,0:T(8,128)(2,1)}, u32[]{:S(2)}, u32[]{:S(2)}) %collective-permute-start.3) | collective-permute-done | bytes 163872 | tf_op jit(solution)/shard_map/ppermute | solution.py:35
  15.2 1.6 order.1.refs_2_
  16.8 1.7 collective-permute-start.4
  18.6 2.2 %collective-permute-start.5 = (bf16[80,4096]{1,0:T(8,128)(2,1)S(1)}, bf16[80,4096]{1,0:T(8,128)(2,1)S(1)}, u32[]{:S(2)}, u32[]{:S(2)}) collective-permute-start(bf16[80,4096]{1,0:T(8,128)(2,1)S(1)} %order.1.refs_2_), channel_id=1, source_target_pairs={{0,3},{1,0},{2,1},{3,2},{4,7},{5,4},{6,5},{7,6},{8,11},{9,8},{10,9... | collective-permute-start | bytes 1966088 | tf_op jit(solution)/shard_map/ppermute | solution.py:86
  21.8 1.7 collective-permute-start.7
  23.5 10.4 %collective-permute-done.4 = bf16[80,4096]{1,0:T(8,128)(2,1)S(1)} collective-permute-done((bf16[80,4096]{1,0:T(8,128)(2,1)S(1)}, bf16[80,4096]{1,0:T(8,128)(2,1)S(1)}, u32[]{:S(2)}, u32[]{:S(2)}) %collective-permute-start.4) | collective-permute-done | bytes 655392 | tf_op jit(solution)/shard_map/ppermute | solution.py:86
  34.1 4.1 %collective-permute-start.8 = (bf16[160,4096]{1,0:T(8,128)(2,1)S(1)}, bf16[160,4096]{1,0:T(8,128)(2,1)}, u32[]{:S(2)}, u32[]{:S(2)}) collective-permute-start(bf16[160,4096]{1,0:T(8,128)(2,1)S(1)} %pad_maximum_fusion.1.refs_3_), channel_id=1, source_target_pairs={{0,24},{1,25},{2,26},{3,27},{4,28},{5,29},{6,30},{7,31},{8,0},{9,1... | collective-permute-start | bytes 3932168 | tf_op jit(solution)/shard_map/ppermute | solution.py:35
  38.2 2.0 %collective-permute-start.10 = (bf16[80,4096]{1,0:T(8,128)(2,1)S(1)}, bf16[80,4096]{1,0:T(8,128)(2,1)}, u32[]{:S(2)}, u32[]{:S(2)}) collective-permute-start(bf16[80,4096]{1,0:T(8,128)(2,1)S(1)} %order.1.refs_2_), channel_id=1, source_target_pairs={{0,2},{1,3},{2,0},{3,1},{4,6},{5,7},{6,4},{7,5},{8,10},{9,11},{10,... | collective-permute-start | bytes 1966088 | tf_op jit(solution)/shard_map/ppermute | solution.py:86
  40.2 9.0 %collective-permute-done.11.refs_6_ = bf16[80,4096]{1,0:T(8,128)(2,1)S(1)} collective-permute-done((bf16[80,4096]{1,0:T(8,128)(2,1)S(1)}, bf16[80,4096]{1,0:T(8,128)(2,1)S(1)}, u32[]{:S(2)}, u32[]{:S(2)}) %collective-permute-start.11) | collective-permute-done | bytes 655392 | tf_op jit(solution)/shard_map/ppermute | solution.py:35
  49.3 6.4 %widen.2.refs_0_ = bf16[768,480]{1,0:T(8,128)(2,1)S(1)} custom-call(bf16[3,128,4096]{2,1,0:T(8,128)(2,1)S(1)} %pad_maximum_fusion.refs_0_.refs_1_, bf16[3,128,4096]{2,1,0:T(8,128)(2,1)} %collective-permute-done.refs_1_.refs_2_, bf16[80,4096]{1,0:T(8,128)(2,1)S(1)} %order.1.refs_2_, bf16[160,4096]{1,0:T(8,128)(2,1)S(1)} %pad_maximum_fusion.1.refs_3_, ...), custom_call_target="tpu_custom_call" | custom-call | flops 3019898880 | bytes 10485760 | tf_op jit(solution)/shard_map/widen/pallas_call | solution.py:217
  56.6 2.7 %collective-permute-start.9 = (bf16[160,4096]{1,0:T(8,128)(2,1)}, bf16[160,4096]{1,0:T(8,128)(2,1)}, u32[]{:S(2)}, u32[]{:S(2)}) collective-permute-start(bf16[160,4096]{1,0:T(8,128)(2,1)} %collective-permute-done.8.refs_4_), channel_id=1, source_target_pairs={{0,24},{1,25},{2,26},{3,27},{4,28},{5,29},{6,30},{7,31},{8,0},{9,1... | collective-permute-start | bytes 3932168 | tf_op jit(solution)/shard_map/ppermute | solution.py:35
  59.7 3.5 %collective-permute-done.14.refs_3_ = bf16[160,4096]{1,0:T(8,128)(2,1)S(1)} collective-permute-done((bf16[160,4096]{1,0:T(8,128)(2,1)S(1)}, bf16[160,4096]{1,0:T(8,128)(2,1)S(1)}, u32[]{:S(2)}, u32[]{:S(2)}) %collective-permute-start.14) | collective-permute-done | bytes 1310752 | tf_op jit(solution)/shard_map/ppermute | solution.py:35
  63.2 6.0 %widen.3.refs_1_ = bf16[768,400]{1,0:T(8,128)(2,1)S(1)} custom-call(bf16[3,128,4096]{2,1,0:T(8,128)(2,1)S(1)} %pad_maximum_fusion.refs_0_.refs_1_, bf16[3,128,4096]{2,1,0:T(8,128)(2,1)} %collective-permute-done.refs_1_.refs_2_, bf16[80,4096]{1,0:T(8,128)(2,1)} %collective-permute-done.10.refs_2_, bf16[160,4096]{1,0:T(8,128)(2,1)S(1)} %collective-permute-done.14.refs_3_, ...), custom_call_target="tpu_custom_call" | custom-call | flops 2516582400 | bytes 10485760 | tf_op jit(solution)/shard_map/widen/pallas_call | solution.py:217
  72.7 3.5 %spread.1.refs_7_ = bf16[64,128,128]{2,1,0:T(8,128)(2,1)S(1)} custom-call(s32[3]{0:T(128)S(1)} %pad_add_fusion.here.refs_0_, bf16[768,480]{1,0:T(8,128)(2,1)S(1)} %copy-done.10, bf16[768,400]{1,0:T(8,128)(2,1)S(1)} %copy-done.7), custom_call_target="tpu_custom_call" | custom-call | flops 1730150400 | bytes 4194304 | tf_op jit(solution)/shard_map/spread/pallas_call | solution.py:195
  76.2 5.5 %collective-permute-done.13.refs_5_ = bf16[80,4096]{1,0:T(8,128)(2,1)} collective-permute-done((bf16[80,4096]{1,0:T(8,128)(2,1)}, bf16[80,4096]{1,0:T(8,128)(2,1)}, u32[]{:S(2)}, u32[]{:S(2)}) %collective-permute-start.13) | collective-permute-done | bytes 655392 | tf_op jit(solution)/shard_map/ppermute | solution.py:35
  81.7 8.9 %widen_last.1 = bf16[64,128,128]{2,1,0:T(8,128)(2,1)S(1)} custom-call(s32[3]{0:T(128)S(1)} %pad_add_fusion.here.refs_0_, bf16[3,128,4096]{2,1,0:T(8,128)(2,1)S(1)} %pad_maximum_fusion.refs_0_.refs_1_, bf16[3,128,4096]{2,1,0:T(8,128)(2,1)} %collective-permute-done.refs_1_.refs_2_, bf16[160,4096]{1,0:T(8,128)(2,1)} %collective-permute-done.9.refs_3_, ...), custom_call_target="tpu_custom_call" | custom-call | flops 3303014400 | bytes 10485760 | tf_op jit(solution)/shard_map/widen_last/pallas_call | solution.py:217
  90.6 1.3 copy-done.1
  91.9 5.3 %all-to-all-start = ((bf16[32,2,128,128]{3,2,1,0:T(8,128)(2,1)}), bf16[32,2,128,128]{3,2,1,0:T(8,128)(2,1)S(1)}, u32[]{:S(2)}, u32[]{:S(2)}) async-start(bf16[32,2,128,128]{3,2,1,0:T(8,128)(2,1)} %bitcast.8), calls=%async_computation | async-start | bytes 4194304 | tf_op jit(solution)/shard_map/all_to_all | solution.py:397
  98.7 20.7 %all-to-all-done.z_ref = bf16[32,2,128,128]{3,2,1,0:T(8,128)(2,1)S(1)} async-done(((bf16[32,2,128,128]{3,2,1,0:T(8,128)(2,1)}), bf16[32,2,128,128]{3,2,1,0:T(8,128)(2,1)S(1)}, u32[]{:S(2)}, u32[]{:S(2)}) %all-to-all-start) | async-done | bytes 2097184 | tf_op jit(solution)/shard_map/all_to_all | solution.py:397
  119.4 1.3 copy-done.2
  120.7 1.6 copy-done.3
  123.4 2.4 %mix.1 = bf16[128,80,128]{2,1,0:T(8,128)(2,1)S(1)} custom-call(bf16[32,2,128,128]{3,2,1,0:T(8,128)(2,1)S(1)} %copy-done.3, bf16[1,640,512]{2,1,0:T(8,128)(2,1)S(1)} %copy-done.5), custom_call_target="tpu_custom_call" | custom-call | flops 1342177280 | bytes 8388608 | tf_op jit(solution)/shard_map/mix/pallas_call | solution.py:301
  125.8 1.5 copy-done
  127.3 14.4 %all-to-all-start.1 = ((bf16[128,80,128]{2,1,0:T(8,128)(2,1)}), bf16[128,80,128]{2,1,0:T(8,128)(2,1)S(1)}, u32[]{:S(2)}, u32[]{:S(2)}) async-start(bf16[128,80,128]{2,1,0:T(8,128)(2,1)} %copy-done), calls=%async_computation.1 | async-start | bytes 5242880 | tf_op jit(solution)/shard_map/all_to_all | solution.py:399
  141.9 35.5 %all-to-all-done.1 = bf16[128,80,128]{2,1,0:T(8,128)(2,1)S(1)} async-done(((bf16[128,80,128]{2,1,0:T(8,128)(2,1)}), bf16[128,80,128]{2,1,0:T(8,128)(2,1)S(1)}, u32[]{:S(2)}, u32[]{:S(2)}) %all-to-all-start.1) | async-done | bytes 2621472 | tf_op jit(solution)/shard_map/all_to_all | solution.py:399
  177.4 4.1 %depth.1 = (bf16[5,40,2560]{2,1,0:T(8,128)(2,1)}, f32[5,40,2560]{2,1,0:T(8,128)}, f32[5,40,2560]{2,1,0:T(8,128)}) custom-call(f32[5,4]{1,0:T(8,128)S(1)} %copy.15.depth, bf16[2,2,32,80,128]{4,3,2,1,0:T(8,128)(2,1)S(1)} %bitcast.7), custom_call_target="tpu_custom_call" | custom-call | flops 12582912 | bytes 8388608 | tf_op jit(solution)/shard_map/depth/pallas_call | solution.py:374
  (54 shorter events, 10.7 us)
Async XLA Ops:
  0.6 2.2 %copy-start.11 = (f32[1,128,4096]{2,1,0:T(8,128)S(1)}, f32[1,128,4096]{2,1,0:T(8,128)}, u32[]{:S(2)}) copy-start(f32[1,128,4096]{2,1,0:T(8,128)} %param.10) | copy-start | bytes 6291460
  2.9 1.2 copy-start.12
  4.1 1.8 %copy-start.8 = (bf16[20,4096]{1,0:T(8,128)(2,1)S(1)}, bf16[20,4096]{1,0:T(8,128)(2,1)}, u32[]{:S(2)}) copy-start(bf16[20,4096]{1,0:T(8,128)(2,1)} %own.1) | copy-start | bytes 491524
  4.4 29.7 %collective-permute-start = (bf16[3,128,4096]{2,1,0:T(8,128)(2,1)S(1)}, bf16[3,128,4096]{2,1,0:T(8,128)(2,1)}, u32[]{:S(2)}, u32[]{:S(2)}) collective-permute-start(bf16[3,128,4096]{2,1,0:T(8,128)(2,1)S(1)} %pad_maximum_fusion.refs_0_.refs_1_), channel_id=1, source_target_pairs={{0,32},{32,0},{1,33},{33,1},{2,34},{34,2},{3,35},{35,3},{4,36},{36... | collective-permute-start | bytes 9437192 | tf_op jit(solution)/shard_map/ppermute | solution.py:90
  5.9 6.0 %collective-permute-start.1 = (bf16[20,4096]{1,0:T(8,128)(2,1)S(1)}, bf16[20,4096]{1,0:T(8,128)(2,1)S(1)}, u32[]{:S(2)}, u32[]{:S(2)}) collective-permute-start(bf16[20,4096]{1,0:T(8,128)(2,1)S(1)} %copy-done.8), channel_id=1, source_target_pairs={{0,4},{1,5},{2,6},{3,7},{4,64},{5,65},{6,66},{7,67},{8,12},{9,13},... | collective-permute-start | bytes 491528 | tf_op jit(solution)/shard_map/ppermute | solution.py:35
  7.2 4.9 %collective-permute-start.2 = (bf16[20,4096]{1,0:T(8,128)(2,1)S(1)}, bf16[20,4096]{1,0:T(8,128)(2,1)}, u32[]{:S(2)}, u32[]{:S(2)}) collective-permute-start(bf16[20,4096]{1,0:T(8,128)(2,1)S(1)} %copy-done.8), channel_id=1, source_target_pairs={{0,68},{1,69},{2,70},{3,71},{4,0},{5,1},{6,2},{7,3},{8,76},{9,77},... | collective-permute-start | bytes 491528 | tf_op jit(solution)/shard_map/ppermute | solution.py:35
  8.6 6.6 %collective-permute-start.3 = (bf16[20,4096]{1,0:T(8,128)(2,1)S(1)}, bf16[20,4096]{1,0:T(8,128)(2,1)}, u32[]{:S(2)}, u32[]{:S(2)}) collective-permute-start(bf16[20,4096]{1,0:T(8,128)(2,1)S(1)} %copy-done.8), channel_id=1, source_target_pairs={{0,64},{1,65},{2,66},{3,67},{4,68},{5,69},{6,70},{7,71},{8,72},{9,... | collective-permute-start | bytes 491528 | tf_op jit(solution)/shard_map/ppermute | solution.py:35
  16.8 17.1 %collective-permute-start.4 = (bf16[80,4096]{1,0:T(8,128)(2,1)S(1)}, bf16[80,4096]{1,0:T(8,128)(2,1)S(1)}, u32[]{:S(2)}, u32[]{:S(2)}) collective-permute-start(bf16[80,4096]{1,0:T(8,128)(2,1)S(1)} %order.1.refs_2_), channel_id=1, source_target_pairs={{0,1},{1,2},{2,3},{3,0},{4,5},{5,6},{6,7},{7,4},{8,9},{9,10},{10,1... | collective-permute-start | bytes 1966088 | tf_op jit(solution)/shard_map/ppermute | solution.py:86
  18.6 15.4 %collective-permute-start.5 = (bf16[80,4096]{1,0:T(8,128)(2,1)S(1)}, bf16[80,4096]{1,0:T(8,128)(2,1)S(1)}, u32[]{:S(2)}, u32[]{:S(2)}) collective-permute-start(bf16[80,4096]{1,0:T(8,128)(2,1)S(1)} %order.1.refs_2_), channel_id=1, source_target_pairs={{0,3},{1,0},{2,1},{3,2},{4,7},{5,4},{6,5},{7,6},{8,11},{9,8},{10,9... | collective-permute-start | bytes 1966088 | tf_op jit(solution)/shard_map/ppermute | solution.py:86
  20.8 13.3 %collective-permute-start.6 = (bf16[80,4096]{1,0:T(8,128)(2,1)S(1)}, bf16[80,4096]{1,0:T(8,128)(2,1)S(1)}, u32[]{:S(2)}, u32[]{:S(2)}) collective-permute-start(bf16[80,4096]{1,0:T(8,128)(2,1)S(1)} %order.1.refs_2_), channel_id=1, source_target_pairs={{0,8},{1,9},{2,10},{3,11},{4,12},{5,13},{6,14},{7,15},{8,16},{9,17... | collective-permute-start | bytes 1966088 | tf_op jit(solution)/shard_map/ppermute | solution.py:35
  21.8 12.3 %collective-permute-start.7 = (bf16[80,4096]{1,0:T(8,128)(2,1)S(1)}, bf16[80,4096]{1,0:T(8,128)(2,1)S(1)}, u32[]{:S(2)}, u32[]{:S(2)}) collective-permute-start(bf16[80,4096]{1,0:T(8,128)(2,1)S(1)} %order.1.refs_2_), channel_id=1, source_target_pairs={{0,24},{1,25},{2,26},{3,27},{4,28},{5,29},{6,30},{7,31},{8,0},{9,1... | collective-permute-start | bytes 1966088 | tf_op jit(solution)/shard_map/ppermute | solution.py:35
  34.1 22.5 %collective-permute-start.8 = (bf16[160,4096]{1,0:T(8,128)(2,1)S(1)}, bf16[160,4096]{1,0:T(8,128)(2,1)}, u32[]{:S(2)}, u32[]{:S(2)}) collective-permute-start(bf16[160,4096]{1,0:T(8,128)(2,1)S(1)} %pad_maximum_fusion.1.refs_3_), channel_id=1, source_target_pairs={{0,24},{1,25},{2,26},{3,27},{4,28},{5,29},{6,30},{7,31},{8,0},{9,1... | collective-permute-start | bytes 3932168 | tf_op jit(solution)/shard_map/ppermute | solution.py:35
  38.2 11.0 %collective-permute-start.11 = (bf16[80,4096]{1,0:T(8,128)(2,1)S(1)}, bf16[80,4096]{1,0:T(8,128)(2,1)S(1)}, u32[]{:S(2)}, u32[]{:S(2)}) collective-permute-start(bf16[80,4096]{1,0:T(8,128)(2,1)S(1)} %collective-permute-done.6.refs_4_), channel_id=1, source_target_pairs={{0,8},{1,9},{2,10},{3,11},{4,12},{5,13},{6,14},{7,15},{8,16},{9,17... | collective-permute-start | bytes 1966088 | tf_op jit(solution)/shard_map/ppermute | solution.py:35
  38.2 25.0 %collective-permute-start.14 = (bf16[160,4096]{1,0:T(8,128)(2,1)S(1)}, bf16[160,4096]{1,0:T(8,128)(2,1)S(1)}, u32[]{:S(2)}, u32[]{:S(2)}) collective-permute-start(bf16[160,4096]{1,0:T(8,128)(2,1)S(1)} %pad_maximum_fusion.1.refs_3_), channel_id=1, source_target_pairs={{0,8},{1,9},{2,10},{3,11},{4,12},{5,13},{6,14},{7,15},{8,16},{9,17... | collective-permute-start | bytes 3932168 | tf_op jit(solution)/shard_map/ppermute | solution.py:35
  38.2 18.3 %collective-permute-start.10 = (bf16[80,4096]{1,0:T(8,128)(2,1)S(1)}, bf16[80,4096]{1,0:T(8,128)(2,1)}, u32[]{:S(2)}, u32[]{:S(2)}) collective-permute-start(bf16[80,4096]{1,0:T(8,128)(2,1)S(1)} %order.1.refs_2_), channel_id=1, source_target_pairs={{0,2},{1,3},{2,0},{3,1},{4,6},{5,7},{6,4},{7,5},{8,10},{9,11},{10,... | collective-permute-start | bytes 1966088 | tf_op jit(solution)/shard_map/ppermute | solution.py:86
  56.6 13.8 %collective-permute-start.12 = (bf16[80,4096]{1,0:T(8,128)(2,1)}, bf16[80,4096]{1,0:T(8,128)(2,1)}, u32[]{:S(2)}, u32[]{:S(2)}) collective-permute-start(bf16[80,4096]{1,0:T(8,128)(2,1)} %collective-permute-done.10.refs_2_), channel_id=1, source_target_pairs={{0,8},{1,9},{2,10},{3,11},{4,12},{5,13},{6,14},{7,15},{8,16},{9,17... | collective-permute-start | bytes 1966088 | tf_op jit(solution)/shard_map/ppermute | solution.py:35
  56.6 25.1 %collective-permute-start.9 = (bf16[160,4096]{1,0:T(8,128)(2,1)}, bf16[160,4096]{1,0:T(8,128)(2,1)}, u32[]{:S(2)}, u32[]{:S(2)}) collective-permute-start(bf16[160,4096]{1,0:T(8,128)(2,1)} %collective-permute-done.8.refs_4_), channel_id=1, source_target_pairs={{0,24},{1,25},{2,26},{3,27},{4,28},{5,29},{6,30},{7,31},{8,0},{9,1... | collective-permute-start | bytes 3932168 | tf_op jit(solution)/shard_map/ppermute | solution.py:35
  59.2 22.5 %collective-permute-start.13 = (bf16[80,4096]{1,0:T(8,128)(2,1)}, bf16[80,4096]{1,0:T(8,128)(2,1)}, u32[]{:S(2)}, u32[]{:S(2)}) collective-permute-start(bf16[80,4096]{1,0:T(8,128)(2,1)} %collective-permute-done.10.refs_2_), channel_id=1, source_target_pairs={{0,24},{1,25},{2,26},{3,27},{4,28},{5,29},{6,30},{7,31},{8,0},{9,1... | collective-permute-start | bytes 1966088 | tf_op jit(solution)/shard_map/ppermute | solution.py:35
  70.3 11.4 %collective-permute-start.15 = (bf16[80,4096]{1,0:T(8,128)(2,1)}, bf16[80,4096]{1,0:T(8,128)(2,1)}, u32[]{:S(2)}, u32[]{:S(2)}) collective-permute-start(bf16[80,4096]{1,0:T(8,128)(2,1)} %collective-permute-done.12.refs_4_), channel_id=1, source_target_pairs={{0,8},{1,9},{2,10},{3,11},{4,12},{5,13},{6,14},{7,15},{8,16},{9,17... | collective-permute-start | bytes 1966088 | tf_op jit(solution)/shard_map/ppermute | solution.py:35
  70.4 1.1 copy-start.7
  71.5 1.1 copy-start.10
  90.6 1.4 copy-start.1
  91.9 5.4 %copy-start.13 = (f32[40,32]{0,1:T(8,128)S(1)}, f32[40,32]{0,1:T(8,128)}, u32[]{:S(2)}) copy-start(f32[40,32]{0,1:T(8,128)} %param.12) | copy-start | bytes 15364
  91.9 27.4 %all-to-all-start = ((bf16[32,2,128,128]{3,2,1,0:T(8,128)(2,1)}), bf16[32,2,128,128]{3,2,1,0:T(8,128)(2,1)S(1)}, u32[]{:S(2)}, u32[]{:S(2)}) async-start(bf16[32,2,128,128]{3,2,1,0:T(8,128)(2,1)} %bitcast.8), calls=%async_computation | async-start | bytes 4194304 | tf_op jit(solution)/shard_map/all_to_all | solution.py:397
  119.4 1.4 copy-start.2
  120.7 1.6 copy-start.3
  122.3 1.1 copy-start.5
  125.8 1.5 copy-start
  127.3 14.4 %copy-start.14 = (f32[5,2]{0,1:T(2,128)S(1)}, f32[5,2]{0,1:T(2,128)}, u32[]{:S(2)}) copy-start(f32[5,2]{0,1:T(2,128)} %param.15) | copy-start | bytes 124
  127.3 14.4 %copy-start.15 = (s32[5,2]{0,1:T(2,128)S(1)}, s32[5,2]{0,1:T(2,128)}, u32[]{:S(2)}) copy-start(s32[5,2]{0,1:T(2,128)} %param.14) | copy-start | bytes 124
  127.3 14.4 %copy-start.16 = (s32[4]{0:T(128)S(1)}, s32[4]{0:T(128)}, u32[]{:S(2)}) copy-start(s32[4]{0:T(128)} %param.13) | copy-start | bytes 52
  127.3 50.1 %all-to-all-start.1 = ((bf16[128,80,128]{2,1,0:T(8,128)(2,1)}), bf16[128,80,128]{2,1,0:T(8,128)(2,1)S(1)}, u32[]{:S(2)}, u32[]{:S(2)}) async-start(bf16[128,80,128]{2,1,0:T(8,128)(2,1)} %copy-done), calls=%async_computation.1 | async-start | bytes 5242880 | tf_op jit(solution)/shard_map/all_to_all | solution.py:399
  (3 other events, 2.6 us)
